TPU v7x, 1024 devices: a whole 4x4x32 slice. The times are simulated.
1024 devices in a mesh: grp: 2 (over x_hi), rep: 64 (over z, x_lo), tp: 8 (over y, core).
Axes of the slice: x: 4 (x_hi: 2, x_lo: 2; x = x_hi * 2 + x_lo), y: 4, z: 32, core: 2. Of those that a mesh axis runs over, the one named last changes fastest.
Arguments:
- grad_parts: float32 [8, 5120, 2048], P('tp', ('grp', 'rep')), may hold values from -124 to 124
- master: float32 [5120, 2048], P(('grp', 'rep'), 'tp'), may hold values from -0.078125 to 0.078125
- moment_one: float32 [5120, 2048], P(('grp', 'rep'), 'tp'), may hold values from -1.5 to 1.5
- moment_two: float32 [5120, 2048], P(('grp', 'rep'), 'tp'), may hold values from 0.003 to 0.03
- hidden_in: bfloat16 [512, 4, 5120], P(('grp', 'rep')), may hold values from -6 to 6
- queries: bfloat16 [512, 4, 5120], P(('grp', 'rep'), None, 'tp'), may hold values from -8 to 8
- cache_keys: bfloat16 [512, 1024, 1024], P(('grp', 'rep'), None, 'tp'), may hold values from -8 to 8
- cache_values: bfloat16 [512, 1024, 1024], P(('grp', 'rep'), None, 'tp'), may hold values from -6 to 6
- cache_lengths: int32 [512], P(('grp', 'rep')), may hold values from 16 to 1024
Outputs:
- new_moment_one: float32 [5120, 2048], P(('grp', 'rep'), 'tp')
- new_moment_two: float32 [5120, 2048], P(('grp', 'rep'), 'tp')
- new_entries: bfloat16 [512, 4, 2048], P(('grp', 'rep'), None, 'tp')
- attended: bfloat16 [512, 4, 5120], P(('grp', 'rep'), None, 'tp')
Inputs may be any that keep to these rules, and one draw needn't show every extreme that they name: `cache_lengths`: cache slots at or after a row's length hold no part of its cache.
All inputs are finite; a program needn't handle non-finite values.
Results may differ from a plain program's by a relative error of at most 0.0051.
Values may be sent and summed in bfloat16 or wider, within the bound.
No kernel may reach another device: no remote copies, remote signals or barrier semaphores. Data moves between devices by JAX's collectives and lax.ppermute only.
A program may use at most 32 MiB of HBM per device.

v0:
```python
import functools
import math

import jax
import jax.numpy as jnp
from jax import lax
from jax.sharding import Mesh
from jax.sharding import PartitionSpec as P

D = 5120
QH = 40
KVH = 8
HD = 128
TP = ("tp_0", "tp_1")
GRP_REP_TP = ("grp", "rep_0", "rep_1", "tp_0", "tp_1")
REP = ("rep_0", "rep_1")
GRP_REP = ("grp", "rep_0", "rep_1")


BETA_ONE = 0.9
BETA_TWO = 0.999
FIRST_CORR = 0.9999734386011124
SECOND_CORR = 0.09520785288629041
LEARN_RATE = 0.003
EPSILON = 1e-08
ROPE_BASE = 1000000.0
NEG_FILL = -1e30


def in_blocks(array, dim, size):
    before, after = (array.shape[:dim], array.shape[dim + 1 :])
    return jnp.moveaxis(array.reshape(*before, size, -1, *after), dim, 0)


def sum_at_owner(array, axis, dim):
    tiles = in_blocks(array, dim, lax.axis_size(axis))
    arrived = lax.all_to_all(tiles, axis, split_axis=0, concat_axis=0, tiled=True)
    return arrived.sum(axis=0)


def by_axis(array, axes):
    return functools.reduce(lax.psum, axes, array)


def from_everyone(array, axis):
    copies = jnp.broadcast_to(array, (lax.axis_size(axis), *array.shape))
    return lax.all_to_all(copies, axis, split_axis=0, concat_axis=0, tiled=True)


def joined_along(tiles, dim):
    shape = list(tiles.shape[1:])
    shape[dim] *= tiles.shape[0]
    return jnp.moveaxis(tiles, 0, dim).reshape(shape)


def gathered_copies(array, axis, dim):
    tiles = from_everyone(array, axis)
    return joined_along(tiles, dim)


def whole_of(array, axes, dim):
    whole = array
    for number in range(len(axes) - 1, -1, -1):
        whole = lax.all_gather(whole, axes[number], axis=dim, tiled=True)
    return whole


def rotate(new_keys, lengths):
    positions = (lengths[:, None] + jnp.arange(new_keys.shape[1], dtype=jnp.int32)[None, :]).astype(
        jnp.float32
    )
    half_dim = new_keys.shape[-1] // 2
    inverse = jnp.exp(
        -math.log(ROPE_BASE) * 2.0 * jnp.arange(half_dim, dtype=jnp.float32) / new_keys.shape[-1]
    )
    angles = positions[:, :, None] * inverse[None, None, :]
    cosine_part = jnp.concatenate([jnp.cos(angles), jnp.cos(angles)], -1)[:, :, None, :]
    sine_part = jnp.concatenate([jnp.sin(angles), jnp.sin(angles)], -1)[:, :, None, :]
    rotated = jnp.concatenate([-new_keys[..., half_dim:], new_keys[..., :half_dim]], -1)
    return new_keys * cosine_part + rotated * sine_part


def body(
    grad_parts,
    master,
    moment_one,
    moment_two,
    hidden_in,
    queries,
    cache_keys,
    cache_values,
    cache_lengths,
):
    col_width = master.shape[1]
    grad_sum = sum_at_owner(grad_parts[0], TP, 1)
    squares = by_axis(jnp.sum(grad_sum * grad_sum), GRP_REP_TP)
    norm_limit = math.sqrt(D * 2 * KVH * HD)
    clipped = grad_sum * jnp.minimum(1.0, norm_limit / jnp.sqrt(squares))
    new_moment_one = BETA_ONE * moment_one + (1.0 - BETA_ONE) * clipped
    new_moment_two = BETA_TWO * moment_two + (1.0 - BETA_TWO) * clipped * clipped
    update = new_moment_one / FIRST_CORR / (jnp.sqrt(new_moment_two / SECOND_CORR) + EPSILON)
    weights = (master - LEARN_RATE * update).astype(jnp.bfloat16)
    row_count, step_count, model_width = hidden_in.shape
    token_count = row_count * step_count
    flat_inputs = hidden_in.reshape(token_count, model_width)
    paired_inputs = gathered_copies(flat_inputs[None], "grp", 0)
    half_offset = lax.axis_index("grp") * (model_width // lax.axis_size("grp"))
    shard_piece = whole_of(weights, REP, 0)
    columns = lax.dynamic_slice_in_dim(paired_inputs, half_offset, shard_piece.shape[0], 2)
    half_terms = jnp.einsum("grn,nc->grc", columns, shard_piece, preferred_element_type=jnp.float32)
    projected = sum_at_owner(half_terms, "grp", 0)[0]
    heads_here = col_width // (2 * HD)
    projected = projected.reshape(row_count, step_count, heads_here, 2, HD)
    new_keys = rotate(projected[:, :, :, 0, :], cache_lengths).astype(jnp.bfloat16)
    new_values = projected[:, :, :, 1, :].astype(jnp.bfloat16)
    new_entries = jnp.stack([new_keys, new_values], 3).reshape(row_count, step_count, col_width)
    groups = QH // KVH
    slots = cache_keys.shape[1]
    query_heads = queries.reshape(row_count, step_count, heads_here, groups, HD)
    old_k = cache_keys.reshape(row_count, slots, heads_here, HD)
    old_v = cache_values.reshape(row_count, slots, heads_here, HD)
    scaling = 1.0 / math.sqrt(HD)
    old_scores = (
        jnp.einsum("rsagd,rjad->rsagj", query_heads, old_k, preferred_element_type=jnp.float32)
        * scaling
    )
    valid_slots = jnp.arange(slots, dtype=jnp.int32)[None, :] < cache_lengths[:, None]
    old_scores = jnp.where(valid_slots[:, None, None, None, :], old_scores, NEG_FILL)
    new_scores = (
        jnp.einsum("rsagd,rtad->rsagt", query_heads, new_keys, preferred_element_type=jnp.float32)
        * scaling
    )
    causal = jnp.arange(step_count)[:, None] >= jnp.arange(step_count)[None, :]
    new_scores = jnp.where(causal[None, :, None, None, :], new_scores, NEG_FILL)
    scores = jnp.concatenate([old_scores, new_scores], -1)
    row_max = jnp.max(scores, -1, keepdims=True)
    exp_scores = jnp.exp(scores - row_max)
    probs = (exp_scores / jnp.sum(exp_scores, -1, keepdims=True)).astype(jnp.bfloat16)
    output = jnp.einsum(
        "rsagj,rjad->rsagd", probs[..., :slots], old_v, preferred_element_type=jnp.float32
    )
    output = output + jnp.einsum(
        "rsagt,rtad->rsagd", probs[..., slots:], new_values, preferred_element_type=jnp.float32
    )
    attended = output.reshape(row_count, step_count, heads_here * groups * HD).astype(jnp.bfloat16)
    return (new_moment_one, new_moment_two, new_entries, attended)


def solution(mesh):
    torus = Mesh(
        mesh.devices.reshape(mesh.shape["grp"], 32, 2, 4, 2),
        ("grp", "rep_0", "rep_1", "tp_0", "tp_1"),
    )
    return jax.shard_map(
        body,
        mesh=torus,
        in_specs=(
            P(TP, GRP_REP, None),
            P(GRP_REP, TP),
            P(GRP_REP, TP),
            P(GRP_REP, TP),
            P(GRP_REP, None, None),
            P(GRP_REP, None, TP),
            P(GRP_REP, None, TP),
            P(GRP_REP, None, TP),
            P(GRP_REP),
        ),
        out_specs=(P(GRP_REP, TP), P(GRP_REP, TP), P(GRP_REP, None, TP), P(GRP_REP, None, TP)),
        check_vma=False,
    )
```

profile of v0, /device:TPU:8, one launch (start us, length us, event | category | flops | bytes accessed | tf_op | source)
XLA Modules:
  0.0 271.7 jit_solution(11448605962143122385)
XLA Ops:
  7.2 0.0 copy-start
  7.2 0.0 copy-start.4
  7.2 0.0 copy-start.5
  7.2 0.0 copy-start.3
  7.2 0.0 all-gather.2.cloned.1.call-start
  7.3 0.0 copy-start.2
  7.3 1.2 copy.41
  8.4 0.1 copy.26
  8.5 0.0 copy-start.6
  8.6 22.3 %all_to_all.15 = f32[8,40,256]{2,1,0:T(8,128)S(1)} all-to-all(f32[8,40,256]{2,1,0:T(8,128)S(1)} %copy.26), channel_id=1, replica_groups=mesh['grp'=2,'rep_0'=32,'rep_1'=2,'tp_0'=4,'tp_1'=2] {'tp_0','tp_1'}, dimensions={0} | all-to-all | bytes 655360 | tf_op jit(solution)/shard_map/all_to_all | solution.py:37
  30.8 0.6 multiply_reduce_fusion
  31.5 7.1 %psum.35 = f32[]{:T(128)} all-reduce(f32[]{:T(128)} %multiply_reduce_fusion), channel_id=1, replica_groups=mesh['grp'=2,'rep_0'=32,'rep_1'=2,'tp_0'=4,'tp_1'=2] {'grp'}, use_global_device_ids=true, to_apply=%region_2.0 | all-reduce | flops 1 | bytes 8 | tf_op jit(solution)/shard_map/psum | solution.py:42
  38.5 59.4 %psum.36 = f32[]{:T(128)} all-reduce(f32[]{:T(128)} %psum.35), channel_id=1, replica_groups=mesh['grp'=2,'rep_0'=32,'rep_1'=2,'tp_0'=4,'tp_1'=2] {'rep_0'}, use_global_device_ids=true, to_apply=%region_3.0 | all-reduce | flops 1 | bytes 8 | tf_op jit(solution)/shard_map/psum | solution.py:42
  97.9 5.5 %psum.37 = f32[]{:T(128)} all-reduce(f32[]{:T(128)} %psum.36), channel_id=1, replica_groups=mesh['grp'=2,'rep_0'=32,'rep_1'=2,'tp_0'=4,'tp_1'=2] {'rep_1'}, use_global_device_ids=true, to_apply=%region_4.0 | all-reduce | flops 1 | bytes 8 | tf_op jit(solution)/shard_map/psum | solution.py:42
  103.4 9.8 %psum.38 = f32[]{:T(128)} all-reduce(f32[]{:T(128)} %psum.37), channel_id=1, replica_groups=mesh['grp'=2,'rep_0'=32,'rep_1'=2,'tp_0'=4,'tp_1'=2] {'tp_0'}, use_global_device_ids=true, to_apply=%region_5.0 | all-reduce | flops 1 | bytes 8 | tf_op jit(solution)/shard_map/psum | solution.py:42
  113.2 3.1 %psum.39 = f32[]{:T(128)} all-reduce(f32[]{:T(128)} %psum.38), channel_id=1, replica_groups=mesh['grp'=2,'rep_0'=32,'rep_1'=2,'tp_0'=4,'tp_1'=2] {'tp_1'}, use_global_device_ids=true, to_apply=%region_6.0 | all-reduce | flops 1 | bytes 8 | tf_op jit(solution)/shard_map/psum | solution.py:42
  117.0 0.0 copy-done.4
  117.0 0.0 copy-done.5
  117.0 0.0 copy-done.3
  117.0 0.7 subtract_convert_fusion
  117.7 4.6 %all_gather.6 = bf16[80,256]{1,0:T(8,128)(2,1)} all-gather(bf16[40,256]{1,0:T(8,128)(2,1)S(1)} %get-tuple-element.4), channel_id=1, replica_groups=mesh['grp'=2,'rep_0'=32,'rep_1'=2,'tp_0'=4,'tp_1'=2] {'rep_1'}, dimensions={0}, use_global_device_ids=true | all-gather | bytes 61440 | tf_op jit(solution)/shard_map/all_gather | solution.py:64
  122.2 0.0 all-gather.2.cloned.1.call-update
  122.2 0.0 copy-done.2
  122.3 0.8 broadcast_in_dim.22
  123.1 4.3 %all-to-all-start.1 = ((bf16[2,1,16,5120]{3,2,1,0:T(8,128)(2,1)}), bf16[2,1,16,5120]{3,2,1,0:T(8,128)(2,1)S(1)}, u32[]{:S(2)}, u32[]{:S(2)}) async-start(bf16[2,1,16,5120]{3,2,1,0:T(8,128)(2,1)} %broadcast_in_dim.22), calls=%async_computation.1 | async-start | bytes 655360 | tf_op jit(solution)/shard_map/all_to_all | solution.py:47
  127.4 0.0 copy-done.6
  127.4 0.0 copy-done.7
  127.4 0.1 add_convert_fusion
  127.5 0.1 iota_compare_fusion
  127.6 0.1 multiply_sine_fusion
  127.7 0.0 copy-done
  127.7 0.5 fusion.33
  128.3 0.1 multiply_cosine_fusion.1
  128.4 6.0 %all-to-all-done.1 = bf16[2,1,16,5120]{3,2,1,0:T(8,128)(2,1)S(1)} async-done(((bf16[2,1,16,5120]{3,2,1,0:T(8,128)(2,1)}), bf16[2,1,16,5120]{3,2,1,0:T(8,128)(2,1)S(1)}, u32[]{:S(2)}, u32[]{:S(2)}) %all-to-all-start.1) | async-done | bytes 327712 | tf_op jit(solution)/shard_map/all_to_all | solution.py:47
  134.4 115.7 %all-gather.2.cloned.1.call-done = bf16[2560,256]{1,0:T(8,128)(2,1)} async-done(((bf16[80,256]{1,0:T(8,128)(2,1)}), bf16[2560,256]{1,0:T(8,128)(2,1)}) %all-gather.2.cloned.1.call-update) | async-done | bytes 1310736 | tf_op jit(solution)/shard_map/all_gather | solution.py:64
  250.1 2.2 fusion.8
  252.3 4.4 %all-to-all-start.2 = ((f32[2,1,16,256]{3,2,1,0:T(8,128)}), f32[2,1,16,256]{3,2,1,0:T(8,128)S(1)}, u32[]{:S(2)}, u32[]{:S(2)}) async-start(f32[2,1,16,256]{3,2,1,0:T(8,128)} %fusion.8), calls=%async_computation.2 | async-start | bytes 65536 | tf_op jit(solution)/shard_map/all_to_all | solution.py:37
  256.7 5.4 %all-to-all-done.2 = f32[2,1,16,256]{3,2,1,0:T(8,128)S(1)} async-done(((f32[2,1,16,256]{3,2,1,0:T(8,128)}), f32[2,1,16,256]{3,2,1,0:T(8,128)S(1)}, u32[]{:S(2)}, u32[]{:S(2)}) %all-to-all-start.2) | async-done | bytes 32800 | tf_op jit(solution)/shard_map/all_to_all | solution.py:37
  262.2 0.1 fusion.23
  262.3 0.3 fusion.34
  262.6 0.3 fusion.15
  262.9 0.2 divide_convert_fusion
  263.1 0.1 fusion.20
  263.2 0.6 copy_bitcast_fusion
  263.8 0.0 copy-done.1
  263.8 0.3 convolution_bitcast_fusion
  264.1 0.1 fusion.11
  264.2 0.6 convert_element_type.62
  (12 shorter events, 0.1 us)
Async XLA Ops:
  7.2 120.5 %copy-start = (bf16[4,1024,128]{2,1,0:T(8,128)(2,1)S(1)}, bf16[4,1024,128]{2,1,0:T(8,128)(2,1)}, u32[]{:S(2)}) copy-start(bf16[4,1024,128]{2,1,0:T(8,128)(2,1)} %param.15) | copy-start | bytes 3145732
  7.2 109.8 %copy-start.4 = (f32[40,256]{1,0:T(8,128)S(1)}, f32[40,256]{1,0:T(8,128)}, u32[]{:S(2)}) copy-start(f32[40,256]{1,0:T(8,128)} %param.12) | copy-start | bytes 122884
  7.2 109.8 %copy-start.5 = (f32[40,256]{1,0:T(8,128)S(1)}, f32[40,256]{1,0:T(8,128)}, u32[]{:S(2)}) copy-start(f32[40,256]{1,0:T(8,128)} %param.11) | copy-start | bytes 122884
  7.2 109.8 %copy-start.3 = (f32[40,256]{1,0:T(8,128)S(1)}, f32[40,256]{1,0:T(8,128)}, u32[]{:S(2)}) copy-start(f32[40,256]{1,0:T(8,128)} %param.10) | copy-start | bytes 122884
  7.2 242.9 %all-gather.2.cloned.1.call-start = ((), (), s32[]{:S(2)}) async-start(), calls=%async_computation.3 | async-start | bytes 1351680 | tf_op jit(solution)/shard_map/all_gather | solution.py:64
  7.3 115.0 %copy-start.2 = (bf16[4,4,5120]{2,1,0:T(4,128)(2,1)S(1)}, bf16[4,4,5120]{2,1,0:T(4,128)(2,1)}, u32[]{:S(2)}) copy-start(bf16[4,4,5120]{2,1,0:T(4,128)(2,1)} %param.13) | copy-start | bytes 491524
  8.5 118.8 %copy-start.6 = (bf16[4,4,640]{2,1,0:T(4,128)(2,1)S(1)}, bf16[4,4,640]{2,1,0:T(4,128)(2,1)}, u32[]{:S(2)}) copy-start(bf16[4,4,640]{2,1,0:T(4,128)(2,1)} %param.14) | copy-start | bytes 61444
  30.8 96.6 %copy-start.7 = (s32[4]{0:T(128)S(1)}, s32[4]{0:T(128)}, u32[]{:S(2)}) copy-start(s32[4]{0:T(128)} %param.17) | copy-start | bytes 52
  123.1 11.3 %all-to-all-start.1 = ((bf16[2,1,16,5120]{3,2,1,0:T(8,128)(2,1)}), bf16[2,1,16,5120]{3,2,1,0:T(8,128)(2,1)S(1)}, u32[]{:S(2)}, u32[]{:S(2)}) async-start(bf16[2,1,16,5120]{3,2,1,0:T(8,128)(2,1)} %broadcast_in_dim.22), calls=%async_computation.1 | async-start | bytes 655360 | tf_op jit(solution)/shard_map/all_to_all | solution.py:47
  252.3 11.5 %copy-start.1 = (bf16[4,1024,128]{2,1,0:T(8,128)(2,1)S(1)}, bf16[4,1024,128]{2,1,0:T(8,128)(2,1)}, u32[]{:S(2)}) copy-start(bf16[4,1024,128]{2,1,0:T(8,128)(2,1)} %param.16) | copy-start | bytes 3145732
  252.3 9.8 %all-to-all-start.2 = ((f32[2,1,16,256]{3,2,1,0:T(8,128)}), f32[2,1,16,256]{3,2,1,0:T(8,128)S(1)}, u32[]{:S(2)}, u32[]{:S(2)}) async-start(f32[2,1,16,256]{3,2,1,0:T(8,128)} %fusion.8), calls=%async_computation.2 | async-start | bytes 65536 | tf_op jit(solution)/shard_map/all_to_all | solution.py:37
Sparse Core Ops, SparseCore 0:
  122.4 127.6 all-gather.1
where the time goes:
time: 272 us
  waiting for transfers between devices  127 us (47%)
  blocking collectives  112 us (41%)
  between operations  14.9 us (5%)
  starting transfers between devices  8.72 us (3%)
  matrix products  3.52 us (1%)
  other arithmetic  2.98 us (1%)
  local copies, waits for them, and re-layouts  2.79 us (1%)
    all_gather x1, waiting for transfers between devices, whole_of(): whole = lax.all_gather(whole, axes[number], axis=dim, tiled=True)  116 us
    psum x5, blocking collectives, by_axis(): return functools.reduce(lax.psum, axes, array)  84.8 us
    all_to_all x1, blocking collectives, sum_at_owner(): lax.all_to_all(tiles, axis, split_axis=0, concat_axis=0, tiled=True)  22.3 us
    all_to_all x1, waiting for transfers between devices, from_everyone(): return lax.all_to_all(copies, axis, split_axis=0, concat_axis=0, tiled=True)  6 us
    all_to_all x1, waiting for transfers between devices, sum_at_owner(): lax.all_to_all(tiles, axis, split_axis=0, concat_axis=0, tiled=True)  5.44 us
  transfers between devices with their start and end apart: 3, of which 3 were waited for; matrix products, arithmetic and copies ran while one was open for 1% of the time, Pallas kernels for 0%

commit v1 on v0

v1 whole, which is shorter than its diff:
```python
import math

import jax
import jax.numpy as jnp
from jax import lax
from jax.experimental import pallas as pl
from jax.experimental.pallas import tpu as pltpu
from jax.sharding import Mesh
from jax.sharding import PartitionSpec as P

D = 5120
QH = 40
KVH = 8
HD = 128
GROUPS = QH // KVH
ZH, ZL = 8, 4
TP = ("y", "c")
REP = ("zh", "zl", "xl")
GRP_REP = ("g",) + REP
SPLIT = ("g", "zl", "xl")
PLANE = ("g", "xl", "y", "c")
LINE = ("zh", "zl")
QROWS = 24

BETA_ONE = 0.9
BETA_TWO = 0.999
FIRST_CORR = 0.9999734386011124
SECOND_CORR = 0.09520785288629041
LEARN_RATE = 0.003
EPSILON = 1e-08
ROPE_BASE = 1000000.0
NEG_FILL = -1e30


def copies_from(array, axes):
    size = math.prod(lax.axis_size(a) for a in axes)
    copies = jnp.broadcast_to(array[None], (size, *array.shape))
    return lax.all_to_all(copies, axes, split_axis=0, concat_axis=0, tiled=True)


def regroup_kernel(x_ref, out_ref):
    x = x_ref[...].astype(jnp.float32)
    step = D // (2 * ZH * ZL * 2)
    for g in range(2):
        for j in range(ZL * 2):
            cols = []
            for zh in range(ZH):
                start = ((g * ZH + zh) * ZL * 2 + j) * step
                cols.append(x[:, start : start + step])
            out_ref[g * ZL * 2 + j] = jnp.concatenate(cols, axis=1).astype(jnp.bfloat16)


def cache_kernel(len_ref, q_ref, k_ref, v_ref, qs_ref, acc_ref, max_ref, sum_ref, qf_ref):
    rows, slots = k_ref.shape[0], k_ref.shape[1]
    steps = q_ref.shape[1]
    qf_ref[...] = jnp.zeros_like(qf_ref)
    for r in range(rows):
        q = q_ref[r].astype(jnp.float32)
        for h in range(GROUPS):
            qf_ref[pl.ds(r * QROWS + h * steps, steps), :] = q[:, h * HD : (h + 1) * HD]
    qs_ref[...] = qf_ref[...].astype(jnp.bfloat16)
    slot = lax.broadcasted_iota(jnp.int32, (QROWS, slots), 1)
    for r in range(rows):
        qb = qf_ref[pl.ds(r * QROWS, QROWS), :].astype(jnp.bfloat16)
        s = lax.dot_general(qb, k_ref[r], (((1,), (1,)), ((), ())), preferred_element_type=jnp.float32)
        s = jnp.where(slot < len_ref[r], s * (1.0 / math.sqrt(HD)), NEG_FILL)
        top = jnp.max(s, axis=1, keepdims=True)
        p = jnp.exp(s - top)
        total = jnp.sum(p, axis=1, keepdims=True)
        acc = jnp.dot(p.astype(jnp.bfloat16), v_ref[r], preferred_element_type=jnp.float32)
        at = pl.ds(r * QROWS, QROWS)
        acc_ref[at, :] = acc
        max_ref[at, :] = jnp.broadcast_to(top, (QROWS, HD))
        sum_ref[at, :] = jnp.broadcast_to(total, (QROWS, HD))


def tail_kernel(part_ref, cos_ref, sin_ref, q_ref, acc_ref, max_ref, sum_ref, new_ref, out_ref, o_ref):
    tokens = part_ref.shape[1]
    rows, steps = out_ref.shape[0], out_ref.shape[1]
    projected = part_ref[0].astype(jnp.float32)
    for i in range(1, part_ref.shape[0]):
        projected = projected + part_ref[i].astype(jnp.float32)
    k, v = projected[:, :HD], projected[:, HD:]
    turned = pltpu.roll(k, HD // 2, 1)
    k = k * cos_ref[...] + turned * sin_ref[...]
    kb, vb = k.astype(jnp.bfloat16), v.astype(jnp.bfloat16)
    new_ref[:, :HD] = kb
    new_ref[:, HD:] = vb
    total_q = q_ref.shape[0]
    s = lax.dot_general(q_ref[...], kb, (((1,), (1,)), ((), ())), preferred_element_type=jnp.float32)
    s = s * (1.0 / math.sqrt(HD))
    q_at = lax.broadcasted_iota(jnp.int32, (total_q, tokens), 0)
    t_at = lax.broadcasted_iota(jnp.int32, (total_q, tokens), 1)
    ok = t_at < 0
    for r in range(rows):
        inside = (q_at >= r * QROWS) & (q_at < (r + 1) * QROWS) & (t_at >= r * steps)
        ok = ok | (inside & (t_at <= r * steps + (q_at & (steps - 1))))
    s = jnp.where(ok, s, NEG_FILL)
    top = jnp.maximum(jnp.max(s, axis=1, keepdims=True), max_ref[...])
    p = jnp.where(ok, jnp.exp(s - top[:, :1]), 0.0)
    fade = jnp.exp(max_ref[...] - top)
    total = sum_ref[...] * fade + jnp.sum(p, axis=1, keepdims=True)
    acc = acc_ref[...] * fade + jnp.dot(p.astype(jnp.bfloat16), vb, preferred_element_type=jnp.float32)
    o_ref[...] = acc / total
    for r in range(rows):
        for h in range(GROUPS):
            out_ref[r, :, h * HD : (h + 1) * HD] = o_ref[pl.ds(r * QROWS + h * steps, steps), :].astype(jnp.bfloat16)


VMEM = pl.BlockSpec(memory_space=pltpu.VMEM)
SMEM = pl.BlockSpec(memory_space=pltpu.SMEM)


def body(grad_parts, master, moment_one, moment_two, hidden_in, queries, cache_keys, cache_values, cache_lengths):
    k_rows, col_width = master.shape
    row_count, step_count, model_width = hidden_in.shape
    tokens = row_count * step_count
    n_split = 2 * ZL * 2
    all_q = row_count * QROWS

    flat = hidden_in.reshape(tokens, model_width)
    blocks = pl.pallas_call(
        regroup_kernel,
        out_shape=jax.ShapeDtypeStruct((n_split, tokens, model_width // n_split), jnp.bfloat16),
        in_specs=[VMEM],
        out_specs=VMEM,
    )(flat)
    inputs = lax.all_to_all(blocks, SPLIT, split_axis=0, concat_axis=0, tiled=True)
    inputs = inputs.reshape(n_split * tokens, model_width // n_split)

    q_rows, old_acc, old_max, old_sum = pl.pallas_call(
        cache_kernel,
        out_shape=(
            jax.ShapeDtypeStruct((all_q, HD), jnp.bfloat16),
            jax.ShapeDtypeStruct((all_q, HD), jnp.float32),
            jax.ShapeDtypeStruct((all_q, HD), jnp.float32),
            jax.ShapeDtypeStruct((all_q, HD), jnp.float32),
        ),
        in_specs=[SMEM, VMEM, VMEM, VMEM],
        out_specs=(VMEM,) * 4,
        scratch_shapes=[pltpu.VMEM((all_q, HD), jnp.float32)],
    )(cache_lengths, queries, cache_keys, cache_values)

    half = HD // 2
    inverse = jnp.exp(-math.log(ROPE_BASE) * 2.0 * jnp.arange(half, dtype=jnp.float32) / HD)
    positions = (cache_lengths[:, None] + jnp.arange(step_count, dtype=jnp.int32)[None, :]).astype(jnp.float32)
    angles = positions.reshape(tokens, 1) * inverse[None, :]
    cosine, sine = jnp.cos(angles), jnp.sin(angles)
    cosine = jnp.concatenate([cosine, cosine], -1)
    sine = jnp.concatenate([-sine, sine], -1)

    tiles = jnp.moveaxis(grad_parts[0].reshape(k_rows, 8, col_width), 1, 0)
    grad_sum = lax.all_to_all(tiles, TP, split_axis=0, concat_axis=0, tiled=True).sum(axis=0)
    squares = jnp.full((1, HD), jnp.sum(grad_sum * grad_sum), jnp.float32)
    squares = copies_from(squares, PLANE).sum(axis=0)
    squares = copies_from(squares, LINE).sum(axis=0)[0, 0]
    norm_limit = math.sqrt(D * 2 * KVH * HD)
    clipped = grad_sum * jnp.minimum(1.0, norm_limit / jnp.sqrt(squares))
    new_moment_one = BETA_ONE * moment_one + (1.0 - BETA_ONE) * clipped
    new_moment_two = BETA_TWO * moment_two + (1.0 - BETA_TWO) * clipped * clipped
    update = new_moment_one / FIRST_CORR / (jnp.sqrt(new_moment_two / SECOND_CORR) + EPSILON)
    weights = (master - LEARN_RATE * update).astype(jnp.bfloat16)

    rows_here = copies_from(weights, ("zh",)).reshape(ZH * k_rows, col_width)
    shares = jnp.dot(inputs, rows_here, preferred_element_type=jnp.float32)
    shares = shares.reshape(n_split, tokens, col_width)
    parts = lax.all_to_all(shares, SPLIT, split_axis=0, concat_axis=0, tiled=True)

    entries, attended = pl.pallas_call(
        tail_kernel,
        out_shape=(
            jax.ShapeDtypeStruct((tokens, col_width), jnp.bfloat16),
            jax.ShapeDtypeStruct((row_count, step_count, GROUPS * HD), jnp.bfloat16),
        ),
        in_specs=[VMEM] * 7,
        out_specs=(VMEM,) * 2,
        scratch_shapes=[pltpu.VMEM((all_q, HD), jnp.float32)],
    )(parts, cosine, sine, q_rows, old_acc, old_max, old_sum)
    return (new_moment_one, new_moment_two, entries.reshape(row_count, step_count, col_width), attended)


def solution(mesh):
    torus = Mesh(mesh.devices.reshape(2, ZH, ZL, 2, 4, 2), ("g", "zh", "zl", "xl", "y", "c"))
    return jax.shard_map(
        body,
        mesh=torus,
        in_specs=(
            P(TP, GRP_REP, None),
            P(GRP_REP, TP),
            P(GRP_REP, TP),
            P(GRP_REP, TP),
            P(GRP_REP, None, None),
            P(GRP_REP, None, TP),
            P(GRP_REP, None, TP),
            P(GRP_REP, None, TP),
            P(GRP_REP),
        ),
        out_specs=(P(GRP_REP, TP), P(GRP_REP, TP), P(GRP_REP, None, TP), P(GRP_REP, None, TP)),
        check_vma=False,
    )
```

time: 272 us -> 145 us (0.53)
  the two profiles are of different devices: /device:TPU:8 before, /device:TPU:2 now
where the time goes in v1:
time: 145 us; the launch traced here: 144 us
  blocking collectives  64.4 us (44%)
  starting transfers between devices  32 us (22%)
  waiting for transfers between devices  31.2 us (22%)
  Pallas kernels  7.55 us (5%)
  local copies, waits for them, and re-layouts  5.29 us (4%)
  other arithmetic  2.2 us (2%)
    all_to_all x2, blocking collectives, copies_from(): return lax.all_to_all(copies, axes, split_axis=0, concat_axis=0, tiled=True)  51.9 us
    all_to_all x1, starting transfers between devices, copies_from(): return lax.all_to_all(copies, axes, split_axis=0, concat_axis=0, tiled=True)  20.1 us
    all_to_all x1, waiting for transfers between devices, copies_from(): return lax.all_to_all(copies, axes, split_axis=0, concat_axis=0, tiled=True)  19.8 us
    all_to_all x1, blocking collectives, body(): lax.all_to_all(tiles, TP, split_axis=0, concat_axis=0, tiled=True)  12.5 us
    all_to_all x1, waiting for transfers between devices, body(): lax.all_to_all(blocks, SPLIT, split_axis=0, concat_axis=0, tiled=True)  7.39 us
    all_to_all x1, starting transfers between devices, body(): lax.all_to_all(shares, SPLIT, split_axis=0, concat_axis=0, tiled=True)  7.04 us
    all_to_all x1, starting transfers between devices, body(): lax.all_to_all(blocks, SPLIT, split_axis=0, concat_axis=0, tiled=True)  4.85 us
    all_to_all x1, waiting for transfers between devices, body(): lax.all_to_all(shares, SPLIT, split_axis=0, concat_axis=0, tiled=True)  4.05 us
  transfers between devices with their start and end apart: 3, of which 3 were waited for; matrix products, arithmetic and copies ran while one was open for 2% of the time, Pallas kernels for 4%

profile of v1, /device:TPU:2, one launch (start us, length us, event | category | flops | bytes accessed | tf_op | source)
XLA Modules:
  0.0 144.4 jit_solution(7194982927700964670)
XLA Ops:
  0.6 1.1 copy.18
  1.7 0.1 copy.15
  1.8 12.5 %all_to_all.30 = f32[8,40,256]{2,1,0:T(8,128)S(1)} all-to-all(f32[8,40,256]{2,1,0:T(8,128)S(1)} %copy.15), channel_id=1, replica_groups=mesh['g'=2,'zh'=8,'zl'=4,'xl'=2,'y'=4,'c'=2] {'y','c'}, dimensions={0} | all-to-all | bytes 655360 | tf_op jit(solution)/shard_map/all_to_all | solution.py:153
  14.3 0.0 copy-start.1
  14.4 0.6 multiply_reduce_fusion
  15.0 0.7 broadcast_in_dim_broadcast_in_dim_broadcast_in_dim.3
  15.6 20.2 %all_to_all.31 = f32[32,1,128]{2,1,0:T(1,128)S(1)} all-to-all(f32[32,1,128]{2,1,0:T(1,128)S(1)} %broadcast_in_dim_broadcast_in_dim_broadcast_in_dim.3), channel_id=1, replica_groups=mesh['g'=2,'zh'=8,'zl'=4,'xl'=2,'y'=4,'c'=2] {'g','xl','y','c'}, dimensions={0} | all-to-all | bytes 32768 | tf_op jit(solution)/shard_map/all_to_all | solution.py:38
  35.9 0.6 broadcast_in_dim.4
  36.5 20.1 %all-to-all-start.2 = ((f32[32,1,128]{2,1,0:T(1,128)}), f32[32,1,128]{2,1,0:T(1,128)S(1)}, u32[]{:S(2)}, u32[]{:S(2)}) async-start(f32[32,1,128]{2,1,0:T(1,128)} %broadcast_in_dim.4), calls=%async_computation.2 | async-start | bytes 32768 | tf_op jit(solution)/shard_map/all_to_all | solution.py:38
  56.6 0.0 copy-done.1
  56.6 0.7 reshape.59.x_ref
  57.3 1.8 %shard_map.120 = bf16[16,16,320]{2,1,0:T(8,128)(2,1)} custom-call(bf16[16,5120]{1,0:T(8,128)(2,1)} %reshape.59.x_ref), custom_call_target="tpu_custom_call" | custom-call | tf_op jit(solution)/shard_map/pallas_call | solution.py:122
  59.1 19.8 %all-to-all-done.2 = f32[32,1,128]{2,1,0:T(1,128)S(1)} async-done(((f32[32,1,128]{2,1,0:T(1,128)}), f32[32,1,128]{2,1,0:T(1,128)S(1)}, u32[]{:S(2)}, u32[]{:S(2)}) %all-to-all-start.2) | async-done | bytes 16416 | tf_op jit(solution)/shard_map/all_to_all | solution.py:38
  78.9 0.0 copy-start.2
  78.9 0.0 copy-start.3
  78.9 0.0 copy-start.4
  78.9 4.9 %all-to-all-start.4 = ((bf16[16,16,320]{2,1,0:T(8,128)(2,1)}), bf16[16,16,320]{2,1,0:T(8,128)(2,1)S(1)}, u32[]{:S(2)}, u32[]{:S(2)}) async-start(bf16[16,16,320]{2,1,0:T(8,128)(2,1)} %shard_map.120), calls=%async_computation.4 | async-start | bytes 393216 | tf_op jit(solution)/shard_map/all_to_all | solution.py:128
  83.9 0.0 copy-done.2
  83.9 0.0 copy-done.3
  83.9 0.0 copy-done.4
  83.9 0.7 subtract_convert_fusion
  84.6 7.4 %all-to-all-done.4 = bf16[16,16,320]{2,1,0:T(8,128)(2,1)S(1)} async-done(((bf16[16,16,320]{2,1,0:T(8,128)(2,1)}), bf16[16,16,320]{2,1,0:T(8,128)(2,1)S(1)}, u32[]{:S(2)}, u32[]{:S(2)}) %all-to-all-start.4) | async-done | bytes 163872 | tf_op jit(solution)/shard_map/all_to_all | solution.py:128
  92.0 31.7 %all_to_all.32 = bf16[8,40,256]{2,1,0:T(8,128)(2,1)S(1)} all-to-all(bf16[8,40,256]{2,1,0:T(8,128)(2,1)S(1)} %broadcast_in_dim.5), channel_id=1, replica_groups=mesh['g'=2,'zh'=8,'zl'=4,'xl'=2,'y'=4,'c'=2] {'zh'}, dimensions={0} | all-to-all | bytes 327680 | tf_op jit(solution)/shard_map/all_to_all | solution.py:38
  123.7 0.9 fusion.3
  124.6 0.0 copy-start.5
  124.6 7.0 %all-to-all-start.5 = ((f32[16,16,256]{2,1,0:T(8,128)}), f32[16,16,256]{2,1,0:T(8,128)S(1)}, u32[]{:S(2)}, u32[]{:S(2)}) async-start(f32[16,16,256]{2,1,0:T(8,128)} %bitcast.8), calls=%async_computation.5 | async-start | bytes 524288 | tf_op jit(solution)/shard_map/all_to_all | solution.py:167
  131.6 0.0 copy-done.5
  131.6 0.1 add_convert_fusion
  131.7 0.1 convert_element_type.15
  131.8 3.6 %shard_map.121 = (bf16[96,128]{1,0:T(8,128)(2,1)}, f32[96,128]{1,0:T(8,128)}, f32[96,128]{1,0:T(8,128)}, f32[96,128]{1,0:T(8,128)}) custom-call(s32[4]{0:T(128)} %len_ref.1, bf16[4,4,640]{2,1,0:T(4,128)(2,1)} %q_ref.1, bf16[4,1024,128]{2,1,0:T(8,128)(2,1)} %k_ref.1, bf16[4,1024,128]{2,1,0:T(8,128)(2,1)} %v_ref.1), custom_call_target="tpu_custom_call" | custom-call | tf_op jit(solution)/shard_map/pallas_call | solution.py:131
  135.4 0.1 fusion.1
  135.5 0.7 pad_maximum_fusion
  136.2 4.0 %all-to-all-done.5.part_ref = f32[16,16,256]{2,1,0:T(8,128)S(1)} async-done(((f32[16,16,256]{2,1,0:T(8,128)}), f32[16,16,256]{2,1,0:T(8,128)S(1)}, u32[]{:S(2)}, u32[]{:S(2)}) %all-to-all-start.5) | async-done | bytes 262176 | tf_op jit(solution)/shard_map/all_to_all | solution.py:167
  140.2 0.0 copy-start
  140.2 0.7 copy-done
  140.9 2.2 %shard_map.122 = (bf16[16,256]{1,0:T(8,128)(2,1)}, bf16[4,4,640]{2,1,0:T(4,128)(2,1)}) custom-call(f32[16,16,256]{2,1,0:T(8,128)} %copy-done, f32[16,128]{1,0:T(8,128)} %get-tuple-element.22.cos_ref, f32[16,128]{1,0:T(8,128)} %get-tuple-element.23.sin_ref, bf16[96,128]{1,0:T(8,128)(2,1)} %get-tuple-element.10.q_ref, f32[96,128]{1,0:T(8,128)} %get-tuple-element.11.acc_ref, ...), custom_call_target="tpu_custom_call" | custom-call | tf_op jit(solution)/shard_map/pallas_call | solution.py:169
  143.1 1.3 reshape.62
  (5 shorter events, 0.1 us)
Async XLA Ops:
  14.3 42.3 %copy-start.1 = (bf16[4,4,5120]{2,1,0:T(4,128)(2,1)S(1)}, bf16[4,4,5120]{2,1,0:T(4,128)(2,1)}, u32[]{:S(2)}) copy-start(bf16[4,4,5120]{2,1,0:T(4,128)(2,1)} %param.13) | copy-start | bytes 491524
  36.5 42.4 %all-to-all-start.2 = ((f32[32,1,128]{2,1,0:T(1,128)}), f32[32,1,128]{2,1,0:T(1,128)S(1)}, u32[]{:S(2)}, u32[]{:S(2)}) async-start(f32[32,1,128]{2,1,0:T(1,128)} %broadcast_in_dim.4), calls=%async_computation.2 | async-start | bytes 32768 | tf_op jit(solution)/shard_map/all_to_all | solution.py:38
  78.9 5.0 %copy-start.2 = (f32[40,256]{1,0:T(8,128)S(1)}, f32[40,256]{1,0:T(8,128)}, u32[]{:S(2)}) copy-start(f32[40,256]{1,0:T(8,128)} %param.10) | copy-start | bytes 122884
  78.9 5.0 %copy-start.3 = (f32[40,256]{1,0:T(8,128)S(1)}, f32[40,256]{1,0:T(8,128)}, u32[]{:S(2)}) copy-start(f32[40,256]{1,0:T(8,128)} %param.12) | copy-start | bytes 122884
  78.9 5.0 %copy-start.4 = (f32[40,256]{1,0:T(8,128)S(1)}, f32[40,256]{1,0:T(8,128)}, u32[]{:S(2)}) copy-start(f32[40,256]{1,0:T(8,128)} %param.11) | copy-start | bytes 122884
  78.9 13.0 %all-to-all-start.4 = ((bf16[16,16,320]{2,1,0:T(8,128)(2,1)}), bf16[16,16,320]{2,1,0:T(8,128)(2,1)S(1)}, u32[]{:S(2)}, u32[]{:S(2)}) async-start(bf16[16,16,320]{2,1,0:T(8,128)(2,1)} %shard_map.120), calls=%async_computation.4 | async-start | bytes 393216 | tf_op jit(solution)/shard_map/all_to_all | solution.py:128
  124.6 7.0 %copy-start.5 = (s32[4]{0:T(128)S(1)}, s32[4]{0:T(128)}, u32[]{:S(2)}) copy-start(s32[4]{0:T(128)} %len_ref.1) | copy-start | bytes 52
  124.6 15.7 %all-to-all-start.5 = ((f32[16,16,256]{2,1,0:T(8,128)}), f32[16,16,256]{2,1,0:T(8,128)S(1)}, u32[]{:S(2)}, u32[]{:S(2)}) async-start(f32[16,16,256]{2,1,0:T(8,128)} %bitcast.8), calls=%async_computation.5 | async-start | bytes 524288 | tf_op jit(solution)/shard_map/all_to_all | solution.py:167
  140.2 0.7 copy-start

commit v2 on v1

--- a/solution.py
+++ b/solution.py
@@ -2,6 +2,7 @@
 
 import jax
 import jax.numpy as jnp
+import numpy as np
 from jax import lax
 from jax.experimental import pallas as pl
 from jax.experimental.pallas import tpu as pltpu
@@ -17,7 +18,7 @@
 TP = ("y", "c")
 REP = ("zh", "zl", "xl")
 GRP_REP = ("g",) + REP
-SPLIT = ("g", "zl", "xl")
+SPLIT = ("zl", "g", "xl")
 PLANE = ("g", "xl", "y", "c")
 LINE = ("zh", "zl")
 QROWS = 24
@@ -38,16 +39,47 @@
     return lax.all_to_all(copies, axes, split_axis=0, concat_axis=0, tiled=True)
 
 
-def regroup_kernel(x_ref, out_ref):
-    x = x_ref[...].astype(jnp.float32)
-    step = D // (2 * ZH * ZL * 2)
-    for g in range(2):
-        for j in range(ZL * 2):
+def near(array):
+    return pltpu.with_memory_space_constraint(array, pltpu.VMEM)
+
+
+def moved(blocks, axes):
+    size = len(blocks)
+    out = [blocks[0]]
+    for k in range(1, size):
+        out.append(near(lax.ppermute(blocks[k], axes, [(i, (i + k) % size) for i in range(size)])))
+    return out
+
+
+def regroup_kernel(at_ref, x_ref, *refs):
+    outs, flat_ref, all_ref = refs[:4], refs[4], refs[5]
+    rows, steps, width = x_ref.shape
+    for r in range(rows):
+        flat_ref[pl.ds(r * steps, steps), :] = x_ref[r].astype(jnp.float32)
+    step = width // (ZH * ZL * 4)
+    for x in range(4):
+        for zl in range(ZL):
             cols = []
             for zh in range(ZH):
-                start = ((g * ZH + zh) * ZL * 2 + j) * step
-                cols.append(x[:, start : start + step])
-            out_ref[g * ZL * 2 + j] = jnp.concatenate(cols, axis=1).astype(jnp.bfloat16)
+                start = (((x // 2 * ZH + zh) * ZL + zl) * 2 + x % 2) * step
+                cols.append(flat_ref[:, start : start + step])
+            all_ref[x, zl] = jnp.concatenate(cols, axis=1).astype(jnp.bfloat16)
+    for k in range(4):
+        outs[k][...] = all_ref[(at_ref[0] + k) & 3]
+
+
+def turn_kernel(at_ref, *refs):
+    for k in range(4):
+        for j in range(4):
+            refs[4 + k][(at_ref[0] - j) & 3] = refs[j][(at_ref[1] + k) & 3]
+
+
+def product_kernel(at_ref, w_ref, *refs):
+    out_ref = refs[4]
+    n, tokens, depth = refs[0].shape
+    for k in range(4):
+        part = jnp.dot(refs[k][...].reshape(n * tokens, depth), w_ref[...], preferred_element_type=jnp.float32)
+        out_ref[(at_ref[1] - k) & 3] = part.reshape(n, tokens, -1)
 
 
 def cache_kernel(len_ref, q_ref, k_ref, v_ref, qs_ref, acc_ref, max_ref, sum_ref, qf_ref):
@@ -74,7 +106,7 @@
         sum_ref[at, :] = jnp.broadcast_to(total, (QROWS, HD))
 
 
-def tail_kernel(part_ref, cos_ref, sin_ref, q_ref, acc_ref, max_ref, sum_ref, new_ref, out_ref, o_ref):
+def tail_kernel(part_ref, cos_ref, sin_ref, q_ref, acc_ref, max_ref, sum_ref, new_ref, out_ref, o_ref, n_ref):
     tokens = part_ref.shape[1]
     rows, steps = out_ref.shape[0], out_ref.shape[1]
     projected = part_ref[0].astype(jnp.float32)
@@ -84,8 +116,10 @@
     turned = pltpu.roll(k, HD // 2, 1)
     k = k * cos_ref[...] + turned * sin_ref[...]
     kb, vb = k.astype(jnp.bfloat16), v.astype(jnp.bfloat16)
-    new_ref[:, :HD] = kb
-    new_ref[:, HD:] = vb
+    n_ref[:, :HD] = k
+    n_ref[:, HD:] = v
+    for r in range(rows):
+        new_ref[r] = n_ref[pl.ds(r * steps, steps), :].astype(jnp.bfloat16)
     total_q = q_ref.shape[0]
     s = lax.dot_general(q_ref[...], kb, (((1,), (1,)), ((), ())), preferred_element_type=jnp.float32)
     s = s * (1.0 / math.sqrt(HD))
@@ -118,15 +152,25 @@
     n_split = 2 * ZL * 2
     all_q = row_count * QROWS
 
-    flat = hidden_in.reshape(tokens, model_width)
-    blocks = pl.pallas_call(
+    tiles = jnp.moveaxis(grad_parts[0].reshape(k_rows, 8, col_width), 1, 0)
+    grad_sum = lax.all_to_all(tiles, TP, split_axis=0, concat_axis=0, tiled=True).sum(axis=0)
+    squares = jnp.sum(grad_sum * grad_sum, axis=0).reshape(2, HD)
+    squares = copies_from(squares, PLANE).sum(axis=0)
+
+    squares, hidden_in, cache_lengths = lax.optimization_barrier((squares, hidden_in, cache_lengths))
+    block = jax.ShapeDtypeStruct((4, tokens, model_width // n_split), jnp.bfloat16)
+    at = jnp.stack([lax.axis_index("g") * 2 + lax.axis_index("xl"), lax.axis_index("zl")]).astype(jnp.int32)
+    along_x = pl.pallas_call(
         regroup_kernel,
-        out_shape=jax.ShapeDtypeStruct((n_split, tokens, model_width // n_split), jnp.bfloat16),
-        in_specs=[VMEM],
-        out_specs=VMEM,
-    )(flat)
-    inputs = lax.all_to_all(blocks, SPLIT, split_axis=0, concat_axis=0, tiled=True)
-    inputs = inputs.reshape(n_split * tokens, model_width // n_split)
+        out_shape=(block,) * 4,
+        in_specs=[SMEM, VMEM],
+        out_specs=(VMEM,) * 4,
+        scratch_shapes=[
+            pltpu.VMEM((tokens, model_width), jnp.float32),
+            pltpu.VMEM((4, ZL, tokens, model_width // n_split), jnp.bfloat16),
+        ],
+    )(at, hidden_in)
+    along_x = moved(along_x, ("g", "xl"))
 
     q_rows, old_acc, old_max, old_sum = pl.pallas_call(
         cache_kernel,
@@ -142,18 +186,20 @@
     )(cache_lengths, queries, cache_keys, cache_values)
 
     half = HD // 2
-    inverse = jnp.exp(-math.log(ROPE_BASE) * 2.0 * jnp.arange(half, dtype=jnp.float32) / HD)
+    inverse = jnp.asarray(ROPE_BASE ** (-2.0 * np.arange(half) / HD), jnp.float32)
     positions = (cache_lengths[:, None] + jnp.arange(step_count, dtype=jnp.int32)[None, :]).astype(jnp.float32)
-    angles = positions.reshape(tokens, 1) * inverse[None, :]
-    cosine, sine = jnp.cos(angles), jnp.sin(angles)
+    turns = positions.reshape(tokens, 1) * inverse[None, :]
+    cosine, sine = jnp.cos(turns), jnp.sin(turns)
     cosine = jnp.concatenate([cosine, cosine], -1)
     sine = jnp.concatenate([-sine, sine], -1)
 
-    tiles = jnp.moveaxis(grad_parts[0].reshape(k_rows, 8, col_width), 1, 0)
-    grad_sum = lax.all_to_all(tiles, TP, split_axis=0, concat_axis=0, tiled=True).sum(axis=0)
-    squares = jnp.full((1, HD), jnp.sum(grad_sum * grad_sum), jnp.float32)
-    squares = copies_from(squares, PLANE).sum(axis=0)
-    squares = copies_from(squares, LINE).sum(axis=0)[0, 0]
+    cached, angles = (q_rows, old_acc, old_max, old_sum), (cosine, sine)
+    squares, along_x, cached, angles = lax.optimization_barrier((copies_from(squares, LINE), along_x, cached, angles))
+    squares = jnp.sum(squares)
+    along_z = pl.pallas_call(turn_kernel, out_shape=(block,) * 4, in_specs=[SMEM] + [VMEM] * 4, out_specs=(VMEM,) * 4)(
+        at, *along_x
+    )
+    inputs = moved(along_z, ("zl",))
     norm_limit = math.sqrt(D * 2 * KVH * HD)
     clipped = grad_sum * jnp.minimum(1.0, norm_limit / jnp.sqrt(squares))
     new_moment_one = BETA_ONE * moment_one + (1.0 - BETA_ONE) * clipped
@@ -161,22 +207,27 @@
     update = new_moment_one / FIRST_CORR / (jnp.sqrt(new_moment_two / SECOND_CORR) + EPSILON)
     weights = (master - LEARN_RATE * update).astype(jnp.bfloat16)
 
-    rows_here = copies_from(weights, ("zh",)).reshape(ZH * k_rows, col_width)
-    shares = jnp.dot(inputs, rows_here, preferred_element_type=jnp.float32)
+    rows_here = near(copies_from(weights, ("zh",)).reshape(ZH * k_rows, col_width))
+    shares = pl.pallas_call(
+        product_kernel,
+        out_shape=jax.ShapeDtypeStruct((ZL, 4, tokens, col_width), jnp.float32),
+        in_specs=[SMEM] + [VMEM] * 5,
+        out_specs=VMEM,
+    )(at, rows_here, *inputs)
     shares = shares.reshape(n_split, tokens, col_width)
     parts = lax.all_to_all(shares, SPLIT, split_axis=0, concat_axis=0, tiled=True)
 
     entries, attended = pl.pallas_call(
         tail_kernel,
         out_shape=(
-            jax.ShapeDtypeStruct((tokens, col_width), jnp.bfloat16),
+            jax.ShapeDtypeStruct((row_count, step_count, col_width), jnp.bfloat16),
             jax.ShapeDtypeStruct((row_count, step_count, GROUPS * HD), jnp.bfloat16),
         ),
         in_specs=[VMEM] * 7,
         out_specs=(VMEM,) * 2,
-        scratch_shapes=[pltpu.VMEM((all_q, HD), jnp.float32)],
-    )(parts, cosine, sine, q_rows, old_acc, old_max, old_sum)
-    return (new_moment_one, new_moment_two, entries.reshape(row_count, step_count, col_width), attended)
+        scratch_shapes=[pltpu.VMEM((all_q, HD), jnp.float32), pltpu.VMEM((tokens, col_width), jnp.float32)],
+    )(near(parts), *angles, *cached)
+    return (new_moment_one, new_moment_two, entries, attended)
 
 
 def solution(mesh):

time: 145 us -> 150 us (1.034)
  blocking collectives: 64.4 us -> 16.3 us
  starting transfers between devices: 32 us -> 72.1 us
  waiting for transfers between devices: 31.2 us -> 41.6 us
  Pallas kernels: 7.55 us -> 10.8 us
    all_to_all x3 -> x1, blocking collectives: 64.4 us -> 16.3 us  [body(): lax.all_to_all(shares, SPLIT, split_axis=0, concat_axis=0, tiled=True)]
    all_to_all x1 -> x3, starting transfers between devices: 20.1 us -> 48.4 us  [copies_from(): return lax.all_to_all(copies, axes, split_axis=0, concat_axis=0, tiled=True)]
    ppermute x0 -> x6, starting transfers between devices: none -> 19.3 us  [moved(): lax.ppermute(blocks[k], axes, [(i, (i + k) % size) for i in range(size)])]
    ppermute x0 -> x6, waiting for transfers between devices: none -> 7.53 us  [moved(): lax.ppermute(blocks[k], axes, [(i, (i + k) % size) for i in range(size)])]
    all_to_all x2 -> x1, starting transfers between devices: 11.9 us -> 4.47 us  [body(): lax.all_to_all(tiles, TP, split_axis=0, concat_axis=0, tiled=True)]
    all_to_all x1 -> x3, waiting for transfers between devices: 19.8 us -> 25.8 us  [copies_from(): return lax.all_to_all(copies, axes, split_axis=0, concat_axis=0, tiled=True)]
    pallas_call x2 -> x4, Pallas kernels: 3.96 us -> 7.18 us  [the longest x1 2.03 us: body(): pl.pallas_call(tail_kernel, out_shape=(jax.ShapeDtypeStruct((row_count, s...]
    all_to_all x2 -> x1, waiting for transfers between devices: 11.4 us -> 8.24 us  [body(): lax.all_to_all(tiles, TP, split_axis=0, concat_axis=0, tiled=True)]
  transfers between devices with their start and end apart: 3 -> 10, of which waited for: 3 -> 6; matrix products, arithmetic and copies ran while one was open for 2% -> 1% of each run, Pallas kernels for 4% -> 5%
where the time goes in v2:
time: 150 us; the launch traced here: 149 us
  starting transfers between devices  72.1 us (48%)
  waiting for transfers between devices  41.6 us (28%)
  blocking collectives  16.3 us (11%)
  Pallas kernels  10.8 us (7%)
  local copies, waits for them, and re-layouts  3.94 us (3%)
  other arithmetic  2.9 us (2%)
    all_to_all x3, starting transfers between devices, copies_from(): return lax.all_to_all(copies, axes, split_axis=0, concat_axis=0, tiled=True)  48.4 us
    all_to_all x3, waiting for transfers between devices, copies_from(): return lax.all_to_all(copies, axes, split_axis=0, concat_axis=0, tiled=True)  25.8 us
    ppermute x6, starting transfers between devices, moved(): lax.ppermute(blocks[k], axes, [(i, (i + k) % size) for i in range(size)])  19.3 us
    all_to_all x1, blocking collectives, body(): lax.all_to_all(shares, SPLIT, split_axis=0, concat_axis=0, tiled=True)  16.3 us
    all_to_all x1, waiting for transfers between devices, body(): lax.all_to_all(tiles, TP, split_axis=0, concat_axis=0, tiled=True)  8.24 us
    ppermute x6, waiting for transfers between devices, moved(): lax.ppermute(blocks[k], axes, [(i, (i + k) % size) for i in range(size)])  7.53 us
    all_to_all x1, starting transfers between devices, body(): lax.all_to_all(tiles, TP, split_axis=0, concat_axis=0, tiled=True)  4.47 us
    pallas_call x1, Pallas kernels, body(): pl.pallas_call(cache_kernel, out_shape=(jax.ShapeDtypeStruct((all_q, HD),...  3.61 us
  transfers between devices with their start and end apart: 10, of which 6 were waited for; matrix products, arithmetic and copies ran while one was open for 1% of the time, Pallas kernels for 5%

profile of v2, /device:TPU:2, one launch (start us, length us, event | category | flops | bytes accessed | tf_op | source)
XLA Modules:
  0.0 149.2 jit_solution(11191160996160154067)
XLA Ops:
  0.6 1.1 copy.19
  1.7 0.8 copy.16
  2.5 4.5 %all-to-all-start = ((f32[8,40,256]{2,1,0:T(8,128)}), f32[8,40,256]{2,1,0:T(8,128)S(1)}, u32[]{:S(2)}, u32[]{:S(2)}) async-start(f32[8,40,256]{2,1,0:T(8,128)} %copy.16), calls=%async_computation | async-start | bytes 655360 | tf_op jit(solution)/shard_map/all_to_all | solution.py:156
  7.0 8.2 %all-to-all-done = f32[8,40,256]{2,1,0:T(8,128)S(1)} async-done(((f32[8,40,256]{2,1,0:T(8,128)}), f32[8,40,256]{2,1,0:T(8,128)S(1)}, u32[]{:S(2)}, u32[]{:S(2)}) %all-to-all-start) | async-done | bytes 327712 | tf_op jit(solution)/shard_map/all_to_all | solution.py:156
  15.3 0.6 broadcast_in_dim.9
  15.9 15.6 %all-to-all-start.1 = ((f32[32,2,128]{2,1,0:T(2,128)}), f32[32,2,128]{2,1,0:T(2,128)S(1)}, u32[]{:S(2)}, u32[]{:S(2)}) async-start(f32[32,2,128]{2,1,0:T(2,128)} %broadcast_in_dim.9), calls=%async_computation.1 | async-start | bytes 65536 | tf_op jit(solution)/shard_map/all_to_all | solution.py:39
  31.6 0.6 pad_add_fusion.at_ref
  32.2 0.0 copy-start.3
  32.2 5.7 %all-to-all-done.1 = f32[32,2,128]{2,1,0:T(2,128)S(1)} async-done(((f32[32,2,128]{2,1,0:T(2,128)}), f32[32,2,128]{2,1,0:T(2,128)S(1)}, u32[]{:S(2)}, u32[]{:S(2)}) %all-to-all-start.1) | async-done | bytes 32800 | tf_op jit(solution)/shard_map/all_to_all | solution.py:39
  37.9 0.0 copy-done.3
  37.9 0.1 add_convert_fusion
  38.0 0.1 convert_element_type.14
  38.1 0.6 broadcast_in_dim.10
  38.7 18.6 %all-to-all-start.2 = ((f32[32,2,128]{2,1,0:T(2,128)}), f32[32,2,128]{2,1,0:T(2,128)S(1)}, u32[]{:S(2)}, u32[]{:S(2)}) async-start(f32[32,2,128]{2,1,0:T(2,128)} %broadcast_in_dim.10), calls=%async_computation.2 | async-start | bytes 65536 | tf_op jit(solution)/shard_map/all_to_all | solution.py:39
  57.3 1.9 %shard_map.129 = (bf16[4,16,320]{2,1,0:T(8,128)(2,1)}, bf16[4,16,320]{2,1,0:T(8,128)(2,1)}, bf16[4,16,320]{2,1,0:T(8,128)(2,1)}, bf16[4,16,320]{2,1,0:T(8,128)(2,1)}) custom-call(s32[2]{0:T(128)} %pad_add_fusion.at_ref, bf16[4,4,5120]{2,1,0:T(4,128)(2,1)} %x_ref), custom_call_target="tpu_custom_call" | custom-call | tf_op jit(solution)/shard_map/pallas_call | solution.py:163
  59.2 2.5 %collective-permute-start = (bf16[4,16,320]{2,1,0:T(8,128)(2,1)}, bf16[4,16,320]{2,1,0:T(8,128)(2,1)S(1)}, u32[]{:S(2)}, u32[]{:S(2)}) collective-permute-start(bf16[4,16,320]{2,1,0:T(8,128)(2,1)} %get-tuple-element.35), channel_id=1, source_target_pairs={{0,8},{8,512},{512,520},{520,0},{1,9},{9,513},{513,521},{521,1},{2... | collective-permute-start | bytes 122888 | tf_op jit(solution)/shard_map/ppermute | solution.py:50
  61.7 0.0 copy-start.4
  61.7 4.8 %collective-permute-start.1 = (bf16[4,16,320]{2,1,0:T(8,128)(2,1)}, bf16[4,16,320]{2,1,0:T(8,128)(2,1)S(1)}, u32[]{:S(2)}, u32[]{:S(2)}) collective-permute-start(bf16[4,16,320]{2,1,0:T(8,128)(2,1)} %get-tuple-element.36), channel_id=1, source_target_pairs={{0,512},{8,520},{512,0},{520,8},{1,513},{9,521},{513,1},{521,9},{2... | collective-permute-start | bytes 122888 | tf_op jit(solution)/shard_map/ppermute | solution.py:50
  66.5 2.5 %collective-permute-start.2 = (bf16[4,16,320]{2,1,0:T(8,128)(2,1)}, bf16[4,16,320]{2,1,0:T(8,128)(2,1)S(1)}, u32[]{:S(2)}, u32[]{:S(2)}) collective-permute-start(bf16[4,16,320]{2,1,0:T(8,128)(2,1)} %get-tuple-element.37), channel_id=1, source_target_pairs={{0,520},{8,0},{512,8},{520,512},{1,521},{9,1},{513,9},{521,513},{2... | collective-permute-start | bytes 122888 | tf_op jit(solution)/shard_map/ppermute | solution.py:50
  69.0 0.0 copy-done.4
  69.0 0.1 fusion.1
  69.1 0.7 pad_maximum_fusion
  69.8 0.0 copy-start.1
  69.8 0.0 copy-start.2
  69.8 3.6 %shard_map.130 = (bf16[96,128]{1,0:T(8,128)(2,1)}, f32[96,128]{1,0:T(8,128)}, f32[96,128]{1,0:T(8,128)}, f32[96,128]{1,0:T(8,128)}) custom-call(s32[4]{0:T(128)} %len_ref, bf16[4,4,640]{2,1,0:T(4,128)(2,1)} %q_ref.1, bf16[4,1024,128]{2,1,0:T(8,128)(2,1)} %k_ref.1, bf16[4,1024,128]{2,1,0:T(8,128)(2,1)} %v_ref.1), custom_call_target="tpu_custom_call" | custom-call | tf_op jit(solution)/shard_map/pallas_call | solution.py:175
  73.4 0.0 copy-start
  73.4 0.0 collective-permute-done.refs_1_
  73.4 0.0 collective-permute-done.1.refs_2_
  73.5 0.0 collective-permute-done.2.refs_3_
  73.5 7.3 %all-to-all-done.2 = f32[32,2,128]{2,1,0:T(2,128)S(1)} async-done(((f32[32,2,128]{2,1,0:T(2,128)}), f32[32,2,128]{2,1,0:T(2,128)S(1)}, u32[]{:S(2)}, u32[]{:S(2)}) %all-to-all-start.2) | async-done | bytes 32800 | tf_op jit(solution)/shard_map/all_to_all | solution.py:39
  80.8 0.6 reduce_sum.39
  82.1 0.0 copy-done.1
  82.1 0.0 copy-done.2
  82.1 0.0 copy-done
  82.1 0.7 subtract_convert_fusion
  82.8 0.7 broadcast_in_dim.11
  83.5 14.1 %all-to-all-start.3 = ((bf16[8,40,256]{2,1,0:T(8,128)(2,1)}), bf16[8,40,256]{2,1,0:T(8,128)(2,1)S(1)}, u32[]{:S(2)}, u32[]{:S(2)}) async-start(bf16[8,40,256]{2,1,0:T(8,128)(2,1)} %broadcast_in_dim.11), calls=%async_computation.3 | async-start | bytes 327680 | tf_op jit(solution)/shard_map/all_to_all | solution.py:39
  97.6 1.5 %shard_map.131 = (bf16[4,16,320]{2,1,0:T(8,128)(2,1)}, bf16[4,16,320]{2,1,0:T(8,128)(2,1)}, bf16[4,16,320]{2,1,0:T(8,128)(2,1)}, bf16[4,16,320]{2,1,0:T(8,128)(2,1)}) custom-call(s32[2]{0:T(128)} %pad_add_fusion.at_ref, bf16[4,16,320]{2,1,0:T(8,128)(2,1)} %get-tuple-element.44.refs_0_, bf16[4,16,320]{2,1,0:T(8,128)(2,1)S(1)} %collective-permute-done.refs_1_, ...), custom_call_target="tpu_custom_call" | custom-call | tf_op jit(solution)/shard_map/pallas_call | solution.py:199
  99.1 2.5 %collective-permute-start.3 = (bf16[4,16,320]{2,1,0:T(8,128)(2,1)}, bf16[4,16,320]{2,1,0:T(8,128)(2,1)S(1)}, u32[]{:S(2)}, u32[]{:S(2)}) collective-permute-start(bf16[4,16,320]{2,1,0:T(8,128)(2,1)} %get-tuple-element.49), channel_id=1, source_target_pairs={{0,16},{16,32},{32,48},{48,0},{1,17},{17,33},{33,49},{49,1},{2,18}... | collective-permute-start | bytes 122888 | tf_op jit(solution)/shard_map/ppermute | solution.py:50
  101.5 2.5 %collective-permute-start.4 = (bf16[4,16,320]{2,1,0:T(8,128)(2,1)}, bf16[4,16,320]{2,1,0:T(8,128)(2,1)S(1)}, u32[]{:S(2)}, u32[]{:S(2)}) collective-permute-start(bf16[4,16,320]{2,1,0:T(8,128)(2,1)} %get-tuple-element.50), channel_id=1, source_target_pairs={{0,32},{16,48},{32,0},{48,16},{1,33},{17,49},{33,1},{49,17},{2,34}... | collective-permute-start | bytes 122888 | tf_op jit(solution)/shard_map/ppermute | solution.py:50
  104.0 4.6 %collective-permute-start.5 = (bf16[4,16,320]{2,1,0:T(8,128)(2,1)}, bf16[4,16,320]{2,1,0:T(8,128)(2,1)S(1)}, u32[]{:S(2)}, u32[]{:S(2)}) collective-permute-start(bf16[4,16,320]{2,1,0:T(8,128)(2,1)} %get-tuple-element.51), channel_id=1, source_target_pairs={{0,48},{16,0},{32,16},{48,32},{1,49},{17,1},{33,17},{49,33},{2,50}... | collective-permute-start | bytes 122888 | tf_op jit(solution)/shard_map/ppermute | solution.py:50
  108.6 4.4 %collective-permute-done.3.refs_1_ = bf16[4,16,320]{2,1,0:T(8,128)(2,1)S(1)} collective-permute-done((bf16[4,16,320]{2,1,0:T(8,128)(2,1)}, bf16[4,16,320]{2,1,0:T(8,128)(2,1)S(1)}, u32[]{:S(2)}, u32[]{:S(2)}) %collective-permute-start.3) | collective-permute-done | bytes 40992 | tf_op jit(solution)/shard_map/ppermute | solution.py:50
  113.0 3.1 %collective-permute-done.4.refs_2_ = bf16[4,16,320]{2,1,0:T(8,128)(2,1)S(1)} collective-permute-done((bf16[4,16,320]{2,1,0:T(8,128)(2,1)}, bf16[4,16,320]{2,1,0:T(8,128)(2,1)S(1)}, u32[]{:S(2)}, u32[]{:S(2)}) %collective-permute-start.4) | collective-permute-done | bytes 40992 | tf_op jit(solution)/shard_map/ppermute | solution.py:50
  116.2 0.0 collective-permute-done.5.refs_3_
  116.2 12.9 %all-to-all-done.3 = bf16[8,40,256]{2,1,0:T(8,128)(2,1)S(1)} async-done(((bf16[8,40,256]{2,1,0:T(8,128)(2,1)}), bf16[8,40,256]{2,1,0:T(8,128)(2,1)S(1)}, u32[]{:S(2)}, u32[]{:S(2)}) %all-to-all-start.3) | async-done | bytes 163872 | tf_op jit(solution)/shard_map/all_to_all | solution.py:39
  129.0 1.8 %shard_map.132 = f32[4,4,16,256]{3,2,1,0:T(8,128)} custom-call(s32[2]{0:T(128)} %pad_add_fusion.at_ref, bf16[320,256]{1,0:T(8,128)(2,1)S(1)} %bitcast.10, bf16[4,16,320]{2,1,0:T(8,128)(2,1)} %get-tuple-element.48.refs_0_, bf16[4,16,320]{2,1,0:T(8,128)(2,1)S(1)} %collective-permute-done.3.refs_1_, bf16[4,16,320]{2,1,0:T(8,128)(2,1)S(1)} %collective-permute-done.4.refs_2_, ...), custom_call_target="tpu_custom_call" | custom-call | tf_op jit(solution)/shard_map/pallas_call | solution.py:211
  130.8 16.3 %all_to_all.25.part_ref = f32[16,16,256]{2,1,0:T(8,128)S(1)} all-to-all(f32[16,16,256]{2,1,0:T(8,128)} %bitcast.12), channel_id=1, replica_groups=mesh['g'=2,'zh'=8,'zl'=4,'xl'=2,'y'=4,'c'=2] {'zl','g','xl'}, dimensions={0} | all-to-all | bytes 524288 | tf_op jit(solution)/shard_map/all_to_all | solution.py:218
  147.1 2.0 %shard_map.133 = (bf16[4,4,256]{2,1,0:T(4,128)(2,1)}, bf16[4,4,640]{2,1,0:T(4,128)(2,1)}) custom-call(f32[16,16,256]{2,1,0:T(8,128)S(1)} %all_to_all.25.part_ref, f32[16,128]{1,0:T(8,128)} %get-tuple-element.52.cos_ref, f32[16,128]{1,0:T(8,128)} %get-tuple-element.53.sin_ref, bf16[96,128]{1,0:T(8,128)(2,1)} %get-tuple-element.54.q_ref, ...), custom_call_target="tpu_custom_call" | custom-call | tf_op jit(solution)/shard_map/pallas_call | solution.py:220
  (3 shorter events, 0.1 us)
Async XLA Ops:
  2.5 12.7 %all-to-all-start = ((f32[8,40,256]{2,1,0:T(8,128)}), f32[8,40,256]{2,1,0:T(8,128)S(1)}, u32[]{:S(2)}, u32[]{:S(2)}) async-start(f32[8,40,256]{2,1,0:T(8,128)} %copy.16), calls=%async_computation | async-start | bytes 655360 | tf_op jit(solution)/shard_map/all_to_all | solution.py:156
  15.9 21.9 %all-to-all-start.1 = ((f32[32,2,128]{2,1,0:T(2,128)}), f32[32,2,128]{2,1,0:T(2,128)S(1)}, u32[]{:S(2)}, u32[]{:S(2)}) async-start(f32[32,2,128]{2,1,0:T(2,128)} %broadcast_in_dim.9), calls=%async_computation.1 | async-start | bytes 65536 | tf_op jit(solution)/shard_map/all_to_all | solution.py:39
  32.2 5.7 %copy-start.3 = (s32[4]{0:T(128)S(1)}, s32[4]{0:T(128)}, u32[]{:S(2)}) copy-start(s32[4]{0:T(128)} %len_ref) | copy-start | bytes 52
  38.7 42.1 %all-to-all-start.2 = ((f32[32,2,128]{2,1,0:T(2,128)}), f32[32,2,128]{2,1,0:T(2,128)S(1)}, u32[]{:S(2)}, u32[]{:S(2)}) async-start(f32[32,2,128]{2,1,0:T(2,128)} %broadcast_in_dim.10), calls=%async_computation.2 | async-start | bytes 65536 | tf_op jit(solution)/shard_map/all_to_all | solution.py:39
  59.2 14.2 %collective-permute-start = (bf16[4,16,320]{2,1,0:T(8,128)(2,1)}, bf16[4,16,320]{2,1,0:T(8,128)(2,1)S(1)}, u32[]{:S(2)}, u32[]{:S(2)}) collective-permute-start(bf16[4,16,320]{2,1,0:T(8,128)(2,1)} %get-tuple-element.35), channel_id=1, source_target_pairs={{0,8},{8,512},{512,520},{520,0},{1,9},{9,513},{513,521},{521,1},{2... | collective-permute-start | bytes 122888 | tf_op jit(solution)/shard_map/ppermute | solution.py:50
  61.7 7.3 %copy-start.4 = (f32[64]{0:T(128)S(1)}, f32[64]{0:T(128)}, u32[]{:S(2)}) copy-start(f32[64]{0:T(128)} %constant.43.clone) | copy-start | bytes 772
  61.7 11.7 %collective-permute-start.1 = (bf16[4,16,320]{2,1,0:T(8,128)(2,1)}, bf16[4,16,320]{2,1,0:T(8,128)(2,1)S(1)}, u32[]{:S(2)}, u32[]{:S(2)}) collective-permute-start(bf16[4,16,320]{2,1,0:T(8,128)(2,1)} %get-tuple-element.36), channel_id=1, source_target_pairs={{0,512},{8,520},{512,0},{520,8},{1,513},{9,521},{513,1},{521,9},{2... | collective-permute-start | bytes 122888 | tf_op jit(solution)/shard_map/ppermute | solution.py:50
  66.5 6.9 %collective-permute-start.2 = (bf16[4,16,320]{2,1,0:T(8,128)(2,1)}, bf16[4,16,320]{2,1,0:T(8,128)(2,1)S(1)}, u32[]{:S(2)}, u32[]{:S(2)}) collective-permute-start(bf16[4,16,320]{2,1,0:T(8,128)(2,1)} %get-tuple-element.37), channel_id=1, source_target_pairs={{0,520},{8,0},{512,8},{520,512},{1,521},{9,1},{513,9},{521,513},{2... | collective-permute-start | bytes 122888 | tf_op jit(solution)/shard_map/ppermute | solution.py:50
  69.8 12.3 %copy-start.1 = (f32[40,256]{1,0:T(8,128)S(1)}, f32[40,256]{1,0:T(8,128)}, u32[]{:S(2)}) copy-start(f32[40,256]{1,0:T(8,128)} %param.13) | copy-start | bytes 122884
  69.8 12.3 %copy-start.2 = (f32[40,256]{1,0:T(8,128)S(1)}, f32[40,256]{1,0:T(8,128)}, u32[]{:S(2)}) copy-start(f32[40,256]{1,0:T(8,128)} %param.12) | copy-start | bytes 122884
  73.4 8.7 %copy-start = (f32[40,256]{1,0:T(8,128)S(1)}, f32[40,256]{1,0:T(8,128)}, u32[]{:S(2)}) copy-start(f32[40,256]{1,0:T(8,128)} %param.11) | copy-start | bytes 122884
  83.5 45.6 %all-to-all-start.3 = ((bf16[8,40,256]{2,1,0:T(8,128)(2,1)}), bf16[8,40,256]{2,1,0:T(8,128)(2,1)S(1)}, u32[]{:S(2)}, u32[]{:S(2)}) async-start(bf16[8,40,256]{2,1,0:T(8,128)(2,1)} %broadcast_in_dim.11), calls=%async_computation.3 | async-start | bytes 327680 | tf_op jit(solution)/shard_map/all_to_all | solution.py:39
  99.1 14.0 %collective-permute-start.3 = (bf16[4,16,320]{2,1,0:T(8,128)(2,1)}, bf16[4,16,320]{2,1,0:T(8,128)(2,1)S(1)}, u32[]{:S(2)}, u32[]{:S(2)}) collective-permute-start(bf16[4,16,320]{2,1,0:T(8,128)(2,1)} %get-tuple-element.49), channel_id=1, source_target_pairs={{0,16},{16,32},{32,48},{48,0},{1,17},{17,33},{33,49},{49,1},{2,18}... | collective-permute-start | bytes 122888 | tf_op jit(solution)/shard_map/ppermute | solution.py:50
  101.5 14.6 %collective-permute-start.4 = (bf16[4,16,320]{2,1,0:T(8,128)(2,1)}, bf16[4,16,320]{2,1,0:T(8,128)(2,1)S(1)}, u32[]{:S(2)}, u32[]{:S(2)}) collective-permute-start(bf16[4,16,320]{2,1,0:T(8,128)(2,1)} %get-tuple-element.50), channel_id=1, source_target_pairs={{0,32},{16,48},{32,0},{48,16},{1,33},{17,49},{33,1},{49,17},{2,34}... | collective-permute-start | bytes 122888 | tf_op jit(solution)/shard_map/ppermute | solution.py:50
  104.0 12.1 %collective-permute-start.5 = (bf16[4,16,320]{2,1,0:T(8,128)(2,1)}, bf16[4,16,320]{2,1,0:T(8,128)(2,1)S(1)}, u32[]{:S(2)}, u32[]{:S(2)}) collective-permute-start(bf16[4,16,320]{2,1,0:T(8,128)(2,1)} %get-tuple-element.51), channel_id=1, source_target_pairs={{0,48},{16,0},{32,16},{48,32},{1,49},{17,1},{33,17},{49,33},{2,50}... | collective-permute-start | bytes 122888 | tf_op jit(solution)/shard_map/ppermute | solution.py:50

commit v3 on v1

--- a/solution.py
+++ b/solution.py
@@ -1,7 +1,9 @@
+import functools
 import math
 
 import jax
 import jax.numpy as jnp
+import numpy as np
 from jax import lax
 from jax.experimental import pallas as pl
 from jax.experimental.pallas import tpu as pltpu
@@ -17,9 +19,8 @@
 TP = ("y", "c")
 REP = ("zh", "zl", "xl")
 GRP_REP = ("g",) + REP
-SPLIT = ("g", "zl", "xl")
-PLANE = ("g", "xl", "y", "c")
-LINE = ("zh", "zl")
+SPLIT = ("zl", "g", "xl")
+ORDER = tuple((i + 5) % ZH for i in range(ZH))
 QROWS = 24
 
 BETA_ONE = 0.9
@@ -32,22 +33,59 @@
 NEG_FILL = -1e30
 
 
-def copies_from(array, axes):
-    size = math.prod(lax.axis_size(a) for a in axes)
-    copies = jnp.broadcast_to(array[None], (size, *array.shape))
-    return lax.all_to_all(copies, axes, split_axis=0, concat_axis=0, tiled=True)
-
-
-def regroup_kernel(x_ref, out_ref):
-    x = x_ref[...].astype(jnp.float32)
-    step = D // (2 * ZH * ZL * 2)
-    for g in range(2):
-        for j in range(ZL * 2):
+def swapped(blocks, axes, groups=None):
+    return lax.all_to_all(blocks, axes, split_axis=0, concat_axis=0, tiled=True, axis_index_groups=groups)
+
+
+def near(array):
+    return pltpu.with_memory_space_constraint(array, pltpu.VMEM)
+
+
+def regroup_kernel(x_ref, out_ref, flat_ref):
+    rows, steps, width = x_ref.shape
+    for r in range(rows):
+        flat_ref[pl.ds(r * steps, steps), :] = x_ref[r].astype(jnp.float32)
+    step = width // (ZH * ZL * 4)
+    room = jnp.zeros((rows * steps, out_ref.shape[2] - ZH * step), jnp.float32)
+    for zl in range(ZL):
+        for x in range(4):
             cols = []
-            for zh in range(ZH):
-                start = ((g * ZH + zh) * ZL * 2 + j) * step
-                cols.append(x[:, start : start + step])
-            out_ref[g * ZL * 2 + j] = jnp.concatenate(cols, axis=1).astype(jnp.bfloat16)
+            for zh in ORDER:
+                start = (((x // 2 * ZH + zh) * ZL + zl) * 2 + x % 2) * step
+                cols.append(flat_ref[:, start : start + step])
+            out_ref[zl * 4 + x] = jnp.concatenate(cols + [room], axis=1).astype(jnp.bfloat16)
+
+
+def norm_kernel(parts_ref, blocks_ref, sum_ref, out_ref, *, width):
+    total = parts_ref[0]
+    for i in range(1, parts_ref.shape[0]):
+        total = total + parts_ref[i]
+    sum_ref[...] = total
+    squares = jnp.sum(jnp.sum(total * total, axis=0, keepdims=True), axis=1, keepdims=True)
+    high = squares.astype(jnp.bfloat16).astype(jnp.float32)
+    rest = squares - high
+    middle = rest.astype(jnp.bfloat16).astype(jnp.float32)
+    low = rest - middle
+    row = lax.broadcasted_iota(jnp.int32, blocks_ref.shape[1:], 0)
+    lane = lax.broadcasted_iota(jnp.int32, blocks_ref.shape[1:], 1)
+    terms = jnp.where(row == 0, high, jnp.where(row == 1, middle, jnp.where(row == 2, low, 0.0)))
+    terms = jnp.where(lane >= width, terms, 0.0).astype(jnp.bfloat16)
+    for i in range(blocks_ref.shape[0]):
+        out_ref[i] = blocks_ref[i] + terms
+
+
+def update_kernel(squares_ref, sum_ref, master_ref, one_ref, two_ref, new_one_ref, new_two_ref, copies_ref):
+    squares = jnp.sum(squares_ref[...], axis=0)
+    scale = jnp.minimum(1.0, math.sqrt(D * 2 * KVH * HD) / jnp.sqrt(squares))[:, :1]
+    clipped = sum_ref[...] * scale
+    one = BETA_ONE * one_ref[...] + (1.0 - BETA_ONE) * clipped
+    two = BETA_TWO * two_ref[...] + (1.0 - BETA_TWO) * clipped * clipped
+    new_one_ref[...] = one
+    new_two_ref[...] = two
+    update = one / FIRST_CORR / (jnp.sqrt(two / SECOND_CORR) + EPSILON)
+    weights = (master_ref[...] - LEARN_RATE * update).astype(jnp.bfloat16)
+    for i in range(copies_ref.shape[0]):
+        copies_ref[i] = weights
 
 
 def cache_kernel(len_ref, q_ref, k_ref, v_ref, qs_ref, acc_ref, max_ref, sum_ref, qf_ref):
@@ -74,7 +112,7 @@
         sum_ref[at, :] = jnp.broadcast_to(total, (QROWS, HD))
 
 
-def tail_kernel(part_ref, cos_ref, sin_ref, q_ref, acc_ref, max_ref, sum_ref, new_ref, out_ref, o_ref):
+def tail_kernel(part_ref, cos_ref, sin_ref, q_ref, acc_ref, max_ref, sum_ref, new_ref, out_ref, o_ref, n_ref):
     tokens = part_ref.shape[1]
     rows, steps = out_ref.shape[0], out_ref.shape[1]
     projected = part_ref[0].astype(jnp.float32)
@@ -84,8 +122,10 @@
     turned = pltpu.roll(k, HD // 2, 1)
     k = k * cos_ref[...] + turned * sin_ref[...]
     kb, vb = k.astype(jnp.bfloat16), v.astype(jnp.bfloat16)
-    new_ref[:, :HD] = kb
-    new_ref[:, HD:] = vb
+    n_ref[:, :HD] = k
+    n_ref[:, HD:] = v
+    for r in range(rows):
+        new_ref[r] = n_ref[pl.ds(r * steps, steps), :].astype(jnp.bfloat16)
     total_q = q_ref.shape[0]
     s = lax.dot_general(q_ref[...], kb, (((1,), (1,)), ((), ())), preferred_element_type=jnp.float32)
     s = s * (1.0 / math.sqrt(HD))
@@ -115,18 +155,36 @@
     k_rows, col_width = master.shape
     row_count, step_count, model_width = hidden_in.shape
     tokens = row_count * step_count
-    n_split = 2 * ZL * 2
+    n_split = 4 * ZL
+    n_tp = 8
+    depth = model_width // n_split
     all_q = row_count * QROWS
 
-    flat = hidden_in.reshape(tokens, model_width)
     blocks = pl.pallas_call(
         regroup_kernel,
-        out_shape=jax.ShapeDtypeStruct((n_split, tokens, model_width // n_split), jnp.bfloat16),
+        out_shape=jax.ShapeDtypeStruct((n_split, tokens, depth + 64), jnp.bfloat16),
         in_specs=[VMEM],
         out_specs=VMEM,
-    )(flat)
-    inputs = lax.all_to_all(blocks, SPLIT, split_axis=0, concat_axis=0, tiled=True)
-    inputs = inputs.reshape(n_split * tokens, model_width // n_split)
+        scratch_shapes=[pltpu.VMEM((tokens, model_width), jnp.float32)],
+    )(hidden_in)
+
+    tiles = jnp.moveaxis(grad_parts[0].reshape(k_rows, n_tp, col_width), 1, 0)
+    arrived = swapped(tiles, TP)
+    grad_sum, blocks = pl.pallas_call(
+        functools.partial(norm_kernel, width=depth),
+        out_shape=(
+            jax.ShapeDtypeStruct((k_rows, col_width), jnp.float32),
+            jax.ShapeDtypeStruct(blocks.shape, jnp.bfloat16),
+        ),
+        in_specs=[VMEM] * 2,
+        out_specs=(VMEM,) * 2,
+    )(near(arrived), near(blocks))
+    blocks = swapped(blocks, SPLIT)
+    squares = jnp.sum(blocks[:, :3, depth].astype(jnp.float32))
+    blocks, squares, cache_lengths = lax.optimization_barrier((blocks, squares, cache_lengths))
+    inputs = blocks[:, :, :depth].reshape(n_split * tokens, depth)
+    peers = [zh * n_tp + t for zh in ORDER for t in range(n_tp)]
+    squares = swapped(jnp.full((ZH * n_tp, 1, HD), squares), ("zh",) + TP, [peers])
 
     q_rows, old_acc, old_max, old_sum = pl.pallas_call(
         cache_kernel,
@@ -142,41 +200,38 @@
     )(cache_lengths, queries, cache_keys, cache_values)
 
     half = HD // 2
-    inverse = jnp.exp(-math.log(ROPE_BASE) * 2.0 * jnp.arange(half, dtype=jnp.float32) / HD)
+    inverse = jnp.asarray(ROPE_BASE ** (-2.0 * np.arange(half) / HD), jnp.float32)
     positions = (cache_lengths[:, None] + jnp.arange(step_count, dtype=jnp.int32)[None, :]).astype(jnp.float32)
-    angles = positions.reshape(tokens, 1) * inverse[None, :]
-    cosine, sine = jnp.cos(angles), jnp.sin(angles)
+    turns = positions.reshape(tokens, 1) * inverse[None, :]
+    cosine, sine = jnp.cos(turns), jnp.sin(turns)
     cosine = jnp.concatenate([cosine, cosine], -1)
     sine = jnp.concatenate([-sine, sine], -1)
 
-    tiles = jnp.moveaxis(grad_parts[0].reshape(k_rows, 8, col_width), 1, 0)
-    grad_sum = lax.all_to_all(tiles, TP, split_axis=0, concat_axis=0, tiled=True).sum(axis=0)
-    squares = jnp.full((1, HD), jnp.sum(grad_sum * grad_sum), jnp.float32)
-    squares = copies_from(squares, PLANE).sum(axis=0)
-    squares = copies_from(squares, LINE).sum(axis=0)[0, 0]
-    norm_limit = math.sqrt(D * 2 * KVH * HD)
-    clipped = grad_sum * jnp.minimum(1.0, norm_limit / jnp.sqrt(squares))
-    new_moment_one = BETA_ONE * moment_one + (1.0 - BETA_ONE) * clipped
-    new_moment_two = BETA_TWO * moment_two + (1.0 - BETA_TWO) * clipped * clipped
-    update = new_moment_one / FIRST_CORR / (jnp.sqrt(new_moment_two / SECOND_CORR) + EPSILON)
-    weights = (master - LEARN_RATE * update).astype(jnp.bfloat16)
-
-    rows_here = copies_from(weights, ("zh",)).reshape(ZH * k_rows, col_width)
-    shares = jnp.dot(inputs, rows_here, preferred_element_type=jnp.float32)
-    shares = shares.reshape(n_split, tokens, col_width)
-    parts = lax.all_to_all(shares, SPLIT, split_axis=0, concat_axis=0, tiled=True)
+
+    square = jax.ShapeDtypeStruct((k_rows, col_width), jnp.float32)
+    new_moment_one, new_moment_two, copies = pl.pallas_call(
+        update_kernel,
+        out_shape=(square, square, jax.ShapeDtypeStruct((ZH, k_rows, col_width), jnp.bfloat16)),
+        in_specs=[VMEM] * 5,
+        out_specs=(VMEM,) * 3,
+    )(near(squares), near(grad_sum), near(master), near(moment_one), near(moment_two))
+    rows_here = swapped(copies, ("zh",), [ORDER])
+    cached, angles = (q_rows, old_acc, old_max, old_sum), (cosine, sine)
+    rows_here, inputs, cached, angles = lax.optimization_barrier((rows_here, inputs, cached, angles))
+    shares = jnp.dot(inputs, rows_here.reshape(ZH * k_rows, col_width), preferred_element_type=jnp.float32)
+    parts = swapped(shares.reshape(n_split, tokens, col_width), SPLIT)
 
     entries, attended = pl.pallas_call(
         tail_kernel,
         out_shape=(
-            jax.ShapeDtypeStruct((tokens, col_width), jnp.bfloat16),
+            jax.ShapeDtypeStruct((row_count, step_count, col_width), jnp.bfloat16),
             jax.ShapeDtypeStruct((row_count, step_count, GROUPS * HD), jnp.bfloat16),
         ),
         in_specs=[VMEM] * 7,
         out_specs=(VMEM,) * 2,
-        scratch_shapes=[pltpu.VMEM((all_q, HD), jnp.float32)],
-    )(parts, cosine, sine, q_rows, old_acc, old_max, old_sum)
-    return (new_moment_one, new_moment_two, entries.reshape(row_count, step_count, col_width), attended)
+        scratch_shapes=[pltpu.VMEM((all_q, HD), jnp.float32), pltpu.VMEM((tokens, col_width), jnp.float32)],
+    )(*[near(array) for array in (parts, *angles, *cached)])
+    return (new_moment_one, new_moment_two, entries, attended)
 
 
 def solution(mesh):

time: 145 us -> 127 us (0.88)
  starting transfers between devices: 32 us -> 21.8 us
  waiting for transfers between devices: 31.2 us -> 21.6 us
  blocking collectives: 64.4 us -> 69.4 us
  local copies, waits for them, and re-layouts: 5.29 us -> 3.62 us
    all_to_all x3 -> x2, starting transfers between devices: 32 us -> 21.8 us  [swapped(): lax.all_to_all(blocks, axes, split_axis=0, concat_axis=0, tiled=True, axi...]
    all_to_all x3 -> x2, waiting for transfers between devices: 31.2 us -> 21.6 us  [swapped(): lax.all_to_all(blocks, axes, split_axis=0, concat_axis=0, tiled=True, axi...]
    all_to_all x3, blocking collectives: 64.4 us -> 69.4 us  [swapped(): lax.all_to_all(blocks, axes, split_axis=0, concat_axis=0, tiled=True, axi...]
    reshape x2 -> x0, local copies, waits for them, and re-layouts: 2.02 us -> none  [the longest x1 1.3 us: body(): entries.reshape(row_count, step_count, col_width)]
  transfers between devices with their start and end apart: 3 -> 2, of which waited for: 3 -> 2; matrix products, arithmetic and copies ran while one was open for 2% -> 0% of each run, Pallas kernels for 4% -> 4%
where the time goes in v3:
time: 127 us
  blocking collectives  69.4 us (55%)
  starting transfers between devices  21.8 us (17%)
  waiting for transfers between devices  21.6 us (17%)
  Pallas kernels  8.23 us (6%)
  local copies, waits for them, and re-layouts  3.62 us (3%)
    all_to_all x3, blocking collectives, swapped(): lax.all_to_all(blocks, axes, split_axis=0, concat_axis=0, tiled=True, axi...  69.4 us
    all_to_all x2, starting transfers between devices, swapped(): lax.all_to_all(blocks, axes, split_axis=0, concat_axis=0, tiled=True, axi...  21.8 us
    all_to_all x2, waiting for transfers between devices, swapped(): lax.all_to_all(blocks, axes, split_axis=0, concat_axis=0, tiled=True, axi...  21.6 us
    pallas_call x1, Pallas kernels, body(): pl.pallas_call(cache_kernel, out_shape=(jax.ShapeDtypeStruct((all_q, HD),...  3.61 us
  transfers between devices with their start and end apart: 2, of which 2 were waited for; matrix products, arithmetic and copies ran while one was open for 0% of the time, Pallas kernels for 4%

profile of v3, /device:TPU:2, one launch (start us, length us, event | category | flops | bytes accessed | tf_op | source)
XLA Modules:
  0.0 126.5 jit_solution(4581013409363431992)
XLA Ops:
  0.6 1.1 copy.15
  1.7 0.8 copy.17
  2.5 4.5 %all-to-all-start = ((f32[8,40,256]{2,1,0:T(8,128)}), f32[8,40,256]{2,1,0:T(8,128)S(1)}, u32[]{:S(2)}, u32[]{:S(2)}) async-start(f32[8,40,256]{2,1,0:T(8,128)} %bitcast.12), calls=%async_computation | async-start | bytes 655360 | tf_op jit(solution)/shard_map/all_to_all | solution.py:37
  7.0 1.8 %shard_map.129.blocks_ref = bf16[16,16,384]{2,1,0:T(8,128)(2,1)} custom-call(bf16[4,4,5120]{2,1,0:T(4,128)(2,1)} %x_ref.1), custom_call_target="tpu_custom_call" | custom-call | tf_op jit(solution)/shard_map/pallas_call | solution.py:163
  8.8 6.4 %all-to-all-done.parts_ref = f32[8,40,256]{2,1,0:T(8,128)S(1)} async-done(((f32[8,40,256]{2,1,0:T(8,128)}), f32[8,40,256]{2,1,0:T(8,128)S(1)}, u32[]{:S(2)}, u32[]{:S(2)}) %all-to-all-start) | async-done | bytes 327712 | tf_op jit(solution)/shard_map/all_to_all | solution.py:37
  15.3 0.0 copy-start
  15.3 0.9 copy-done
  16.2 0.8 shard_map.130
  17.0 0.0 copy-start.6
  17.0 0.0 copy-start.7
  17.0 23.7 %all_to_all.25 = bf16[16,16,384]{2,1,0:T(8,128)(2,1)S(1)} all-to-all(bf16[16,16,384]{2,1,0:T(8,128)(2,1)} %get-tuple-element.26), channel_id=1, replica_groups=mesh['g'=2,'zh'=8,'zl'=4,'xl'=2,'y'=4,'c'=2] {'zl','g','xl'}, dimensions={0} | all-to-all | bytes 393216 | tf_op jit(solution)/shard_map/all_to_all | solution.py:37
  40.7 0.0 copy-start.5
  40.7 0.7 convert_reduce_fusion
  41.4 0.7 broadcast_in_dim.2
  42.0 0.0 copy-start.4
  42.0 32.1 %all_to_all.26.squares_ref = f32[64,1,128]{2,1,0:T(1,128)S(1)} all-to-all(f32[64,1,128]{2,1,0:T(1,128)S(1)} %broadcast_in_dim.2), channel_id=1, replica_groups={{320,321,322,323,324,325,326,327,384,385,386,387,388,389,390,391,448,44..., dimensions={0} | all-to-all | bytes 65536 | tf_op jit(solution)/shard_map/all_to_all | solution.py:37
  74.2 0.0 copy-done.6
  74.2 0.0 copy-done.7
  74.2 0.0 copy-done.5
  74.2 0.0 copy-done.4
  74.2 0.8 shard_map.131
  75.0 0.0 copy-start.9
  75.0 17.3 %all-to-all-start.3 = ((bf16[8,40,256]{2,1,0:T(8,128)(2,1)}), bf16[8,40,256]{2,1,0:T(8,128)(2,1)S(1)}, u32[]{:S(2)}, u32[]{:S(2)}) async-start(bf16[8,40,256]{2,1,0:T(8,128)(2,1)} %get-tuple-element.31), calls=%async_computation.3 | async-start | bytes 327680 | tf_op jit(solution)/shard_map/all_to_all | solution.py:37
  92.3 0.0 copy-done.9
  92.3 0.1 add_convert_fusion
  92.4 0.1 convert_element_type.16
  92.5 0.0 copy-start.10
  92.5 3.6 %shard_map.132 = (bf16[96,128]{1,0:T(8,128)(2,1)}, f32[96,128]{1,0:T(8,128)}, f32[96,128]{1,0:T(8,128)}, f32[96,128]{1,0:T(8,128)}) custom-call(s32[4]{0:T(128)} %len_ref, bf16[4,4,640]{2,1,0:T(4,128)(2,1)} %q_ref.1, bf16[4,1024,128]{2,1,0:T(8,128)(2,1)} %k_ref.1, bf16[4,1024,128]{2,1,0:T(8,128)(2,1)} %v_ref.1), custom_call_target="tpu_custom_call" | custom-call | tf_op jit(solution)/shard_map/pallas_call | solution.py:189
  96.1 0.0 copy-done.10
  96.1 0.1 fusion
  96.2 0.1 pad_maximum_fusion
  96.3 15.2 %all-to-all-done.3 = bf16[8,40,256]{2,1,0:T(8,128)(2,1)S(1)} async-done(((bf16[8,40,256]{2,1,0:T(8,128)(2,1)}), bf16[8,40,256]{2,1,0:T(8,128)(2,1)S(1)}, u32[]{:S(2)}, u32[]{:S(2)}) %all-to-all-start.3) | async-done | bytes 163872 | tf_op jit(solution)/shard_map/all_to_all | solution.py:37
  111.5 0.2 fusion.1
  111.7 0.0 copy-start.1
  111.7 0.0 copy-start.2
  111.7 0.0 copy-start.3
  111.7 0.0 copy-start.8
  111.7 13.6 %all_to_all.27.part_ref = f32[16,16,256]{2,1,0:T(8,128)S(1)} all-to-all(f32[16,16,256]{2,1,0:T(8,128)S(1)} %fusion.1), channel_id=1, replica_groups=mesh['g'=2,'zh'=8,'zl'=4,'xl'=2,'y'=4,'c'=2] {'zl','g','xl'}, dimensions={0} | all-to-all | bytes 524288 | tf_op jit(solution)/shard_map/all_to_all | solution.py:37
  125.4 0.0 copy-done.1
  125.4 0.0 copy-done.2
  125.4 0.0 copy-done.3
  125.4 0.0 copy-done.8
  125.4 1.1 shard_map.133
Async XLA Ops:
  2.5 12.7 %all-to-all-start = ((f32[8,40,256]{2,1,0:T(8,128)}), f32[8,40,256]{2,1,0:T(8,128)S(1)}, u32[]{:S(2)}, u32[]{:S(2)}) async-start(f32[8,40,256]{2,1,0:T(8,128)} %bitcast.12), calls=%async_computation | async-start | bytes 655360 | tf_op jit(solution)/shard_map/all_to_all | solution.py:37
  15.3 0.9 copy-start
  17.0 57.2 %copy-start.6 = (f32[40,256]{1,0:T(8,128)S(1)}, f32[40,256]{1,0:T(8,128)}, u32[]{:S(2)}) copy-start(f32[40,256]{1,0:T(8,128)} %two_ref.1) | copy-start | bytes 122884
  17.0 57.2 %copy-start.7 = (f32[40,256]{1,0:T(8,128)S(1)}, f32[40,256]{1,0:T(8,128)}, u32[]{:S(2)}) copy-start(f32[40,256]{1,0:T(8,128)} %get-tuple-element.28.sum_ref) | copy-start | bytes 122884
  40.7 33.5 %copy-start.5 = (f32[40,256]{1,0:T(8,128)S(1)}, f32[40,256]{1,0:T(8,128)}, u32[]{:S(2)}) copy-start(f32[40,256]{1,0:T(8,128)} %one_ref.1) | copy-start | bytes 122884
  42.0 32.1 %copy-start.4 = (f32[40,256]{1,0:T(8,128)S(1)}, f32[40,256]{1,0:T(8,128)}, u32[]{:S(2)}) copy-start(f32[40,256]{1,0:T(8,128)} %master_ref.1) | copy-start | bytes 122884
  75.0 17.3 %copy-start.9 = (s32[4]{0:T(128)S(1)}, s32[4]{0:T(128)}, u32[]{:S(2)}) copy-start(s32[4]{0:T(128)} %len_ref) | copy-start | bytes 52
  75.0 36.5 %all-to-all-start.3 = ((bf16[8,40,256]{2,1,0:T(8,128)(2,1)}), bf16[8,40,256]{2,1,0:T(8,128)(2,1)S(1)}, u32[]{:S(2)}, u32[]{:S(2)}) async-start(bf16[8,40,256]{2,1,0:T(8,128)(2,1)} %get-tuple-element.31), calls=%async_computation.3 | async-start | bytes 327680 | tf_op jit(solution)/shard_map/all_to_all | solution.py:37
  92.5 3.6 %copy-start.10 = (f32[64]{0:T(128)S(1)}, f32[64]{0:T(128)}, u32[]{:S(2)}) copy-start(f32[64]{0:T(128)} %constant.4.clone) | copy-start | bytes 772
  111.7 13.7 %copy-start.1 = (f32[96,128]{1,0:T(8,128)S(1)}, f32[96,128]{1,0:T(8,128)}, u32[]{:S(2)}) copy-start(f32[96,128]{1,0:T(8,128)} %get-tuple-element.43.acc_ref) | copy-start | bytes 147460
  111.7 13.7 %copy-start.2 = (f32[96,128]{1,0:T(8,128)S(1)}, f32[96,128]{1,0:T(8,128)}, u32[]{:S(2)}) copy-start(f32[96,128]{1,0:T(8,128)} %get-tuple-element.44.max_ref) | copy-start | bytes 147460
  111.7 13.7 %copy-start.3 = (f32[96,128]{1,0:T(8,128)S(1)}, f32[96,128]{1,0:T(8,128)}, u32[]{:S(2)}) copy-start(f32[96,128]{1,0:T(8,128)} %get-tuple-element.45.sum_ref) | copy-start | bytes 147460
  111.7 13.7 %copy-start.8 = (bf16[96,128]{1,0:T(8,128)(2,1)S(1)}, bf16[96,128]{1,0:T(8,128)(2,1)}, u32[]{:S(2)}) copy-start(bf16[96,128]{1,0:T(8,128)(2,1)} %get-tuple-element.42.q_ref) | copy-start | bytes 73732

commit v4 on v3

--- a/solution.py
+++ b/solution.py
@@ -41,22 +41,7 @@
     return pltpu.with_memory_space_constraint(array, pltpu.VMEM)
 
 
-def regroup_kernel(x_ref, out_ref, flat_ref):
-    rows, steps, width = x_ref.shape
-    for r in range(rows):
-        flat_ref[pl.ds(r * steps, steps), :] = x_ref[r].astype(jnp.float32)
-    step = width // (ZH * ZL * 4)
-    room = jnp.zeros((rows * steps, out_ref.shape[2] - ZH * step), jnp.float32)
-    for zl in range(ZL):
-        for x in range(4):
-            cols = []
-            for zh in ORDER:
-                start = (((x // 2 * ZH + zh) * ZL + zl) * 2 + x % 2) * step
-                cols.append(flat_ref[:, start : start + step])
-            out_ref[zl * 4 + x] = jnp.concatenate(cols + [room], axis=1).astype(jnp.bfloat16)
-
-
-def norm_kernel(parts_ref, blocks_ref, sum_ref, out_ref, *, width):
+def norm_kernel(parts_ref, x_ref, sum_ref, out_ref, flat_ref):
     total = parts_ref[0]
     for i in range(1, parts_ref.shape[0]):
         total = total + parts_ref[i]
@@ -66,12 +51,30 @@
     rest = squares - high
     middle = rest.astype(jnp.bfloat16).astype(jnp.float32)
     low = rest - middle
-    row = lax.broadcasted_iota(jnp.int32, blocks_ref.shape[1:], 0)
-    lane = lax.broadcasted_iota(jnp.int32, blocks_ref.shape[1:], 1)
+    rows, steps, width = x_ref.shape
+    for r in range(rows):
+        flat_ref[pl.ds(r * steps, steps), :] = x_ref[r].astype(jnp.float32)
+    step = width // (ZH * ZL * 4)
+    row = lax.broadcasted_iota(jnp.int32, (rows * steps, out_ref.shape[2] - ZH * step), 0)
     terms = jnp.where(row == 0, high, jnp.where(row == 1, middle, jnp.where(row == 2, low, 0.0)))
-    terms = jnp.where(lane >= width, terms, 0.0).astype(jnp.bfloat16)
-    for i in range(blocks_ref.shape[0]):
-        out_ref[i] = blocks_ref[i] + terms
+    for zl in range(ZL):
+        for x in range(4):
+            cols = []
+            for zh in ORDER:
+                start = (((x // 2 * ZH + zh) * ZL + zl) * 2 + x % 2) * step
+                cols.append(flat_ref[:, start : start + step])
+            out_ref[zl * 4 + x] = jnp.concatenate(cols + [terms], axis=1).astype(jnp.bfloat16)
+
+
+def share_kernel(blocks_ref, squares_ref, inputs_ref):
+    n, tokens, _ = blocks_ref.shape
+    depth = inputs_ref.shape[1]
+    terms = blocks_ref[:, :, 256:384].astype(jnp.float32)
+    total = jnp.sum(jnp.sum(terms, axis=0), axis=0, keepdims=True)
+    total = jnp.broadcast_to(total[:, depth - 256 : depth - 255], (1, squares_ref.shape[2]))
+    for i in range(squares_ref.shape[0]):
+        squares_ref[i] = total
+    inputs_ref[...] = blocks_ref[:, :, :depth].reshape(n * tokens, depth)
 
 
 def update_kernel(squares_ref, sum_ref, master_ref, one_ref, two_ref, new_one_ref, new_two_ref, copies_ref):
@@ -160,31 +163,30 @@
     depth = model_width // n_split
     all_q = row_count * QROWS
 
-    blocks = pl.pallas_call(
-        regroup_kernel,
-        out_shape=jax.ShapeDtypeStruct((n_split, tokens, depth + 64), jnp.bfloat16),
-        in_specs=[VMEM],
-        out_specs=VMEM,
-        scratch_shapes=[pltpu.VMEM((tokens, model_width), jnp.float32)],
-    )(hidden_in)
-
     tiles = jnp.moveaxis(grad_parts[0].reshape(k_rows, n_tp, col_width), 1, 0)
     arrived = swapped(tiles, TP)
     grad_sum, blocks = pl.pallas_call(
-        functools.partial(norm_kernel, width=depth),
+        norm_kernel,
         out_shape=(
             jax.ShapeDtypeStruct((k_rows, col_width), jnp.float32),
-            jax.ShapeDtypeStruct(blocks.shape, jnp.bfloat16),
+            jax.ShapeDtypeStruct((n_split, tokens, depth + 64), jnp.bfloat16),
         ),
         in_specs=[VMEM] * 2,
         out_specs=(VMEM,) * 2,
-    )(near(arrived), near(blocks))
-    blocks = swapped(blocks, SPLIT)
-    squares = jnp.sum(blocks[:, :3, depth].astype(jnp.float32))
-    blocks, squares, cache_lengths = lax.optimization_barrier((blocks, squares, cache_lengths))
-    inputs = blocks[:, :, :depth].reshape(n_split * tokens, depth)
+        scratch_shapes=[pltpu.VMEM((tokens, model_width), jnp.float32)],
+    )(near(arrived), near(hidden_in))
+    squares, inputs = pl.pallas_call(
+        share_kernel,
+        out_shape=(
+            jax.ShapeDtypeStruct((ZH * n_tp, 1, HD), jnp.float32),
+            jax.ShapeDtypeStruct((n_split * tokens, depth), jnp.bfloat16),
+        ),
+        in_specs=[VMEM],
+        out_specs=(VMEM,) * 2,
+    )(near(swapped(blocks, SPLIT)))
+    inputs, squares, cache_lengths = lax.optimization_barrier((inputs, squares, cache_lengths))
     peers = [zh * n_tp + t for zh in ORDER for t in range(n_tp)]
-    squares = swapped(jnp.full((ZH * n_tp, 1, HD), squares), ("zh",) + TP, [peers])
+    squares = swapped(squares, ("zh",) + TP, [peers])
 
     q_rows, old_acc, old_max, old_sum = pl.pallas_call(
         cache_kernel,

time: 127 us -> 125 us (0.984)
  blocking collectives: 69.4 us -> 82.4 us
  waiting for transfers between devices: 21.6 us -> 15.4 us
  starting transfers between devices: 21.8 us -> 17 us
  local copies, waits for them, and re-layouts: 3.62 us -> 1.32 us
    all_to_all x3 -> x4, blocking collectives: 69.4 us -> 82.4 us  [swapped(): lax.all_to_all(blocks, axes, split_axis=0, concat_axis=0, tiled=True, axi...]
    all_to_all x2 -> x1, waiting for transfers between devices: 21.6 us -> 15.4 us  [swapped(): lax.all_to_all(blocks, axes, split_axis=0, concat_axis=0, tiled=True, axi...]
    all_to_all x2 -> x1, starting transfers between devices: 21.8 us -> 17 us  [swapped(): lax.all_to_all(blocks, axes, split_axis=0, concat_axis=0, tiled=True, axi...]
  transfers between devices with their start and end apart: 2 -> 1, of which waited for: 2 -> 1; matrix products, arithmetic and copies ran while one was open for 0% -> 0% of each run, Pallas kernels for 4% -> 3%
where the time goes in v4:
time: 125 us
  blocking collectives  82.4 us (66%)
  starting transfers between devices  17 us (14%)
  waiting for transfers between devices  15.4 us (12%)
  Pallas kernels  7.27 us (6%)
  local copies, waits for them, and re-layouts  1.32 us (1%)
    all_to_all x4, blocking collectives, swapped(): lax.all_to_all(blocks, axes, split_axis=0, concat_axis=0, tiled=True, axi...  82.4 us
    all_to_all x1, starting transfers between devices, swapped(): lax.all_to_all(blocks, axes, split_axis=0, concat_axis=0, tiled=True, axi...  17 us
    all_to_all x1, waiting for transfers between devices, swapped(): lax.all_to_all(blocks, axes, split_axis=0, concat_axis=0, tiled=True, axi...  15.4 us
    pallas_call x1, Pallas kernels, body(): pl.pallas_call(cache_kernel, out_shape=(jax.ShapeDtypeStruct((all_q, HD),...  3.63 us
  transfers between devices with their start and end apart: 1, of which 1 were waited for; matrix products, arithmetic and copies ran while one was open for 0% of the time, Pallas kernels for 3%

profile of v4, /device:TPU:2, one launch (start us, length us, event | category | flops | bytes accessed | tf_op | source)
XLA Modules:
  0.0 124.6 jit_solution(7763465722276560719)
XLA Ops:
  0.6 1.1 copy.15
  1.7 0.1 copy.17
  1.8 0.0 copy-start
  1.8 12.6 %all_to_all.25.parts_ref = f32[8,40,256]{2,1,0:T(8,128)S(1)} all-to-all(f32[8,40,256]{2,1,0:T(8,128)S(1)} %bitcast.12), channel_id=1, replica_groups=mesh['g'=2,'zh'=8,'zl'=4,'xl'=2,'y'=4,'c'=2] {'y','c'}, dimensions={0} | all-to-all | bytes 655360 | tf_op jit(solution)/shard_map/all_to_all | solution.py:37
  14.5 0.0 copy-done
  14.5 0.9 shard_map.129
  15.4 23.1 %all_to_all.26.blocks_ref = bf16[16,16,384]{2,1,0:T(8,128)(2,1)S(1)} all-to-all(bf16[16,16,384]{2,1,0:T(8,128)(2,1)} %get-tuple-element.28), channel_id=1, replica_groups=mesh['g'=2,'zh'=8,'zl'=4,'xl'=2,'y'=4,'c'=2] {'zl','g','xl'}, dimensions={0} | all-to-all | bytes 393216 | tf_op jit(solution)/shard_map/all_to_all | solution.py:37
  38.6 0.0 copy-start.5
  38.6 0.0 copy-start.6
  38.6 0.0 copy-start.7
  38.6 0.7 shard_map.130
  39.3 0.0 copy-start.4
  39.3 33.2 %all_to_all.27.squares_ref = f32[64,1,128]{2,1,0:T(1,128)S(1)} all-to-all(f32[64,1,128]{2,1,0:T(1,128)} %get-tuple-element.31), channel_id=1, replica_groups={{320,321,322,323,324,325,326,327,384,385,386,387,388,389,390,391,448,44..., dimensions={0} | all-to-all | bytes 65536 | tf_op jit(solution)/shard_map/all_to_all | solution.py:37
  72.5 0.0 copy-done.5
  72.5 0.0 copy-done.6
  72.5 0.0 copy-done.7
  72.5 0.0 copy-done.4
  72.5 0.8 shard_map.131
  73.4 0.0 copy-start.10
  73.4 17.0 %all-to-all-start.3 = ((bf16[8,40,256]{2,1,0:T(8,128)(2,1)}), bf16[8,40,256]{2,1,0:T(8,128)(2,1)S(1)}, u32[]{:S(2)}, u32[]{:S(2)}) async-start(bf16[8,40,256]{2,1,0:T(8,128)(2,1)} %get-tuple-element.35), calls=%async_computation.3 | async-start | bytes 327680 | tf_op jit(solution)/shard_map/all_to_all | solution.py:37
  90.3 0.0 copy-done.10
  90.3 0.1 add_convert_fusion
  90.4 0.1 convert_element_type.11
  90.5 0.0 copy-start.11
  90.5 0.0 copy-start.9
  90.5 3.6 %shard_map.132 = (bf16[96,128]{1,0:T(8,128)(2,1)}, f32[96,128]{1,0:T(8,128)}, f32[96,128]{1,0:T(8,128)}, f32[96,128]{1,0:T(8,128)}) custom-call(s32[4]{0:T(128)} %len_ref, bf16[4,4,640]{2,1,0:T(4,128)(2,1)} %q_ref.1, bf16[4,1024,128]{2,1,0:T(8,128)(2,1)} %k_ref.1, bf16[4,1024,128]{2,1,0:T(8,128)(2,1)} %v_ref.1), custom_call_target="tpu_custom_call" | custom-call | tf_op jit(solution)/shard_map/pallas_call | solution.py:191
  94.1 0.0 copy-done.11
  94.1 0.1 fusion
  94.3 0.1 pad_maximum_fusion
  94.3 15.4 %all-to-all-done.3 = bf16[8,40,256]{2,1,0:T(8,128)(2,1)S(1)} async-done(((bf16[8,40,256]{2,1,0:T(8,128)(2,1)}), bf16[8,40,256]{2,1,0:T(8,128)(2,1)S(1)}, u32[]{:S(2)}, u32[]{:S(2)}) %all-to-all-start.3) | async-done | bytes 163872 | tf_op jit(solution)/shard_map/all_to_all | solution.py:37
  109.7 0.0 copy-done.9
  109.7 0.2 fusion.1
  109.9 0.0 copy-start.1
  109.9 0.0 copy-start.2
  109.9 0.0 copy-start.3
  110.0 0.0 copy-start.8
  110.0 13.4 %all_to_all.28.part_ref = f32[16,16,256]{2,1,0:T(8,128)S(1)} all-to-all(f32[16,16,256]{2,1,0:T(8,128)S(1)} %fusion.1), channel_id=1, replica_groups=mesh['g'=2,'zh'=8,'zl'=4,'xl'=2,'y'=4,'c'=2] {'zl','g','xl'}, dimensions={0} | all-to-all | bytes 524288 | tf_op jit(solution)/shard_map/all_to_all | solution.py:37
  123.4 0.0 copy-done.1
  123.4 0.0 copy-done.2
  123.4 0.0 copy-done.3
  123.4 0.0 copy-done.8
  123.4 1.1 shard_map.133
Async XLA Ops:
  1.8 12.7 %copy-start = (bf16[4,4,5120]{2,1,0:T(4,128)(2,1)S(1)}, bf16[4,4,5120]{2,1,0:T(4,128)(2,1)}, u32[]{:S(2)}) copy-start(bf16[4,4,5120]{2,1,0:T(4,128)(2,1)} %x_ref.1) | copy-start | bytes 491524
  38.6 34.0 %copy-start.5 = (f32[40,256]{1,0:T(8,128)S(1)}, f32[40,256]{1,0:T(8,128)}, u32[]{:S(2)}) copy-start(f32[40,256]{1,0:T(8,128)} %one_ref.1) | copy-start | bytes 122884
  38.6 34.0 %copy-start.6 = (f32[40,256]{1,0:T(8,128)S(1)}, f32[40,256]{1,0:T(8,128)}, u32[]{:S(2)}) copy-start(f32[40,256]{1,0:T(8,128)} %two_ref.1) | copy-start | bytes 122884
  38.6 34.0 %copy-start.7 = (f32[40,256]{1,0:T(8,128)S(1)}, f32[40,256]{1,0:T(8,128)}, u32[]{:S(2)}) copy-start(f32[40,256]{1,0:T(8,128)} %get-tuple-element.32.sum_ref) | copy-start | bytes 122884
  39.3 33.2 %copy-start.4 = (f32[40,256]{1,0:T(8,128)S(1)}, f32[40,256]{1,0:T(8,128)}, u32[]{:S(2)}) copy-start(f32[40,256]{1,0:T(8,128)} %master_ref.1) | copy-start | bytes 122884
  73.4 17.0 %copy-start.10 = (s32[4]{0:T(128)S(1)}, s32[4]{0:T(128)}, u32[]{:S(2)}) copy-start(s32[4]{0:T(128)} %len_ref) | copy-start | bytes 52
  73.4 36.3 %all-to-all-start.3 = ((bf16[8,40,256]{2,1,0:T(8,128)(2,1)}), bf16[8,40,256]{2,1,0:T(8,128)(2,1)S(1)}, u32[]{:S(2)}, u32[]{:S(2)}) async-start(bf16[8,40,256]{2,1,0:T(8,128)(2,1)} %get-tuple-element.35), calls=%async_computation.3 | async-start | bytes 327680 | tf_op jit(solution)/shard_map/all_to_all | solution.py:37
  90.5 3.6 %copy-start.11 = (f32[64]{0:T(128)S(1)}, f32[64]{0:T(128)}, u32[]{:S(2)}) copy-start(f32[64]{0:T(128)} %constant.2.clone) | copy-start | bytes 772
  90.5 19.2 %copy-start.9 = (bf16[256,320]{1,0:T(8,128)(2,1)S(1)}, bf16[256,320]{1,0:T(8,128)(2,1)}, u32[]{:S(2)}) copy-start(bf16[256,320]{1,0:T(8,128)(2,1)} %get-tuple-element.42) | copy-start | bytes 491524
  109.9 13.5 %copy-start.1 = (f32[96,128]{1,0:T(8,128)S(1)}, f32[96,128]{1,0:T(8,128)}, u32[]{:S(2)}) copy-start(f32[96,128]{1,0:T(8,128)} %get-tuple-element.47.acc_ref) | copy-start | bytes 147460
  109.9 13.5 %copy-start.2 = (f32[96,128]{1,0:T(8,128)S(1)}, f32[96,128]{1,0:T(8,128)}, u32[]{:S(2)}) copy-start(f32[96,128]{1,0:T(8,128)} %get-tuple-element.48.max_ref) | copy-start | bytes 147460
  109.9 13.5 %copy-start.3 = (f32[96,128]{1,0:T(8,128)S(1)}, f32[96,128]{1,0:T(8,128)}, u32[]{:S(2)}) copy-start(f32[96,128]{1,0:T(8,128)} %get-tuple-element.49.sum_ref) | copy-start | bytes 147460
  110.0 13.4 %copy-start.8 = (bf16[96,128]{1,0:T(8,128)(2,1)S(1)}, bf16[96,128]{1,0:T(8,128)(2,1)}, u32[]{:S(2)}) copy-start(bf16[96,128]{1,0:T(8,128)(2,1)} %get-tuple-element.46.q_ref) | copy-start | bytes 73732

commit v5 on v4

--- a/solution.py
+++ b/solution.py
@@ -20,7 +20,9 @@
 REP = ("zh", "zl", "xl")
 GRP_REP = ("g",) + REP
 SPLIT = ("zl", "g", "xl")
-ORDER = tuple((i + 5) % ZH for i in range(ZH))
+ORDER = (5, 4, 0, 1, 2, 6, 7, 3)
+NORM_ORDER = tuple(zh * 8 + t for zh in ORDER for t in range(8))
+SPLIT_ORDER = tuple(range(15, -1, -1))
 QROWS = 24
 
 BETA_ONE = 0.9
@@ -63,7 +65,7 @@
             for zh in ORDER:
                 start = (((x // 2 * ZH + zh) * ZL + zl) * 2 + x % 2) * step
                 cols.append(flat_ref[:, start : start + step])
-            out_ref[zl * 4 + x] = jnp.concatenate(cols + [terms], axis=1).astype(jnp.bfloat16)
+            out_ref[SPLIT_ORDER.index(zl * 4 + x)] = jnp.concatenate(cols + [terms], axis=1).astype(jnp.bfloat16)
 
 
 def share_kernel(blocks_ref, squares_ref, inputs_ref):
@@ -183,10 +185,9 @@
         ),
         in_specs=[VMEM],
         out_specs=(VMEM,) * 2,
-    )(near(swapped(blocks, SPLIT)))
+    )(near(swapped(blocks, SPLIT, [SPLIT_ORDER])))
     inputs, squares, cache_lengths = lax.optimization_barrier((inputs, squares, cache_lengths))
-    peers = [zh * n_tp + t for zh in ORDER for t in range(n_tp)]
-    squares = swapped(squares, ("zh",) + TP, [peers])
+    squares = swapped(squares, ("zh",) + TP, [NORM_ORDER])
 
     q_rows, old_acc, old_max, old_sum = pl.pallas_call(
         cache_kernel,
@@ -221,7 +222,7 @@
     cached, angles = (q_rows, old_acc, old_max, old_sum), (cosine, sine)
     rows_here, inputs, cached, angles = lax.optimization_barrier((rows_here, inputs, cached, angles))
     shares = jnp.dot(inputs, rows_here.reshape(ZH * k_rows, col_width), preferred_element_type=jnp.float32)
-    parts = swapped(shares.reshape(n_split, tokens, col_width), SPLIT)
+    parts = swapped(shares.reshape(n_split, tokens, col_width), SPLIT, [SPLIT_ORDER])
 
     entries, attended = pl.pallas_call(
         tail_kernel,

time: 125 us -> 122 us (0.976)
  the two profiles are of different devices: /device:TPU:2 before, /device:TPU:1 now
where the time goes in v5:
time: 122 us
  blocking collectives  84.8 us (70%)
  starting transfers between devices  17.8 us (15%)
  waiting for transfers between devices  9.38 us (8%)
  Pallas kernels  7.27 us (6%)
  local copies, waits for them, and re-layouts  1.32 us (1%)
    all_to_all x4, blocking collectives, swapped(): lax.all_to_all(blocks, axes, split_axis=0, concat_axis=0, tiled=True, axi...  84.8 us
    all_to_all x1, starting transfers between devices, swapped(): lax.all_to_all(blocks, axes, split_axis=0, concat_axis=0, tiled=True, axi...  17.8 us
    all_to_all x1, waiting for transfers between devices, swapped(): lax.all_to_all(blocks, axes, split_axis=0, concat_axis=0, tiled=True, axi...  9.38 us
    pallas_call x1, Pallas kernels, body(): pl.pallas_call(cache_kernel, out_shape=(jax.ShapeDtypeStruct((all_q, HD),...  3.63 us
  transfers between devices with their start and end apart: 1, of which 1 were waited for; matrix products, arithmetic and copies ran while one was open for 0% of the time, Pallas kernels for 3%

profile of v5, /device:TPU:1, one launch (start us, length us, event | category | flops | bytes accessed | tf_op | source)
XLA Modules:
  0.0 121.8 jit_solution(3845028786299575836)
XLA Ops:
  0.6 1.1 copy.15
  1.7 0.1 copy.17
  1.8 0.0 copy-start
  1.8 24.2 %all_to_all.25.parts_ref = f32[8,40,256]{2,1,0:T(8,128)S(1)} all-to-all(f32[8,40,256]{2,1,0:T(8,128)S(1)} %bitcast.12), channel_id=1, replica_groups=mesh['g'=2,'zh'=8,'zl'=4,'xl'=2,'y'=4,'c'=2] {'y','c'}, dimensions={0} | all-to-all | bytes 655360 | tf_op jit(solution)/shard_map/all_to_all | solution.py:39
  26.0 0.0 copy-done
  26.0 0.9 shard_map.129
  26.9 12.1 %all_to_all.26.blocks_ref = bf16[16,16,384]{2,1,0:T(8,128)(2,1)S(1)} all-to-all(bf16[16,16,384]{2,1,0:T(8,128)(2,1)} %get-tuple-element.28), channel_id=1, replica_groups={{568,560,56,48,552,544,40,32,536,528,24,16,520,512,8,0},{569,561,57,49,..., dimensions={0} | all-to-all | bytes 393216 | tf_op jit(solution)/shard_map/all_to_all | solution.py:39
  39.1 0.0 copy-start.5
  39.1 0.0 copy-start.6
  39.1 0.0 copy-start.7
  39.1 0.7 shard_map.130
  39.8 0.0 copy-start.4
  39.8 31.2 %all_to_all.27.squares_ref = f32[64,1,128]{2,1,0:T(1,128)S(1)} all-to-all(f32[64,1,128]{2,1,0:T(1,128)} %get-tuple-element.31), channel_id=1, replica_groups={{320,321,322,323,324,325,326,327,256,257,258,259,260,261,262,263,0,1,2,..., dimensions={0} | all-to-all | bytes 65536 | tf_op jit(solution)/shard_map/all_to_all | solution.py:39
  71.0 0.0 copy-done.5
  71.0 0.0 copy-done.6
  71.0 0.0 copy-done.7
  71.0 0.0 copy-done.4
  71.0 0.8 shard_map.131
  71.9 0.0 copy-start.10
  71.9 17.8 %all-to-all-start.3 = ((bf16[8,40,256]{2,1,0:T(8,128)(2,1)}), bf16[8,40,256]{2,1,0:T(8,128)(2,1)S(1)}, u32[]{:S(2)}, u32[]{:S(2)}) async-start(bf16[8,40,256]{2,1,0:T(8,128)(2,1)} %get-tuple-element.35), calls=%async_computation.3 | async-start | bytes 327680 | tf_op jit(solution)/shard_map/all_to_all | solution.py:39
  89.7 0.0 copy-done.10
  89.7 0.1 add_convert_fusion
  89.8 0.1 convert_element_type.11
  89.8 0.0 copy-start.11
  89.8 0.0 copy-start.9
  89.9 3.6 %shard_map.132 = (bf16[96,128]{1,0:T(8,128)(2,1)}, f32[96,128]{1,0:T(8,128)}, f32[96,128]{1,0:T(8,128)}, f32[96,128]{1,0:T(8,128)}) custom-call(s32[4]{0:T(128)} %len_ref, bf16[4,4,640]{2,1,0:T(4,128)(2,1)} %q_ref.1, bf16[4,1024,128]{2,1,0:T(8,128)(2,1)} %k_ref.1, bf16[4,1024,128]{2,1,0:T(8,128)(2,1)} %v_ref.1), custom_call_target="tpu_custom_call" | custom-call | tf_op jit(solution)/shard_map/pallas_call | solution.py:192
  93.5 0.0 copy-done.11
  93.5 0.1 fusion
  93.6 0.1 pad_maximum_fusion
  93.7 9.4 %all-to-all-done.3 = bf16[8,40,256]{2,1,0:T(8,128)(2,1)S(1)} async-done(((bf16[8,40,256]{2,1,0:T(8,128)(2,1)}), bf16[8,40,256]{2,1,0:T(8,128)(2,1)S(1)}, u32[]{:S(2)}, u32[]{:S(2)}) %all-to-all-start.3) | async-done | bytes 163872 | tf_op jit(solution)/shard_map/all_to_all | solution.py:39
  103.1 0.0 copy-done.9
  103.1 0.2 fusion.1
  103.3 0.0 copy-start.1
  103.3 0.0 copy-start.2
  103.3 0.0 copy-start.3
  103.3 0.0 copy-start.8
  103.3 17.3 %all_to_all.28.part_ref = f32[16,16,256]{2,1,0:T(8,128)S(1)} all-to-all(f32[16,16,256]{2,1,0:T(8,128)S(1)} %fusion.1), channel_id=1, replica_groups={{568,560,56,48,552,544,40,32,536,528,24,16,520,512,8,0},{569,561,57,49,..., dimensions={0} | all-to-all | bytes 524288 | tf_op jit(solution)/shard_map/all_to_all | solution.py:39
  120.6 0.0 copy-done.1
  120.6 0.0 copy-done.2
  120.6 0.0 copy-done.3
  120.6 0.0 copy-done.8
  120.6 1.1 shard_map.133
Async XLA Ops:
  1.8 24.2 %copy-start = (bf16[4,4,5120]{2,1,0:T(4,128)(2,1)S(1)}, bf16[4,4,5120]{2,1,0:T(4,128)(2,1)}, u32[]{:S(2)}) copy-start(bf16[4,4,5120]{2,1,0:T(4,128)(2,1)} %x_ref.1) | copy-start | bytes 491524
  39.1 32.0 %copy-start.5 = (f32[40,256]{1,0:T(8,128)S(1)}, f32[40,256]{1,0:T(8,128)}, u32[]{:S(2)}) copy-start(f32[40,256]{1,0:T(8,128)} %one_ref.1) | copy-start | bytes 122884
  39.1 32.0 %copy-start.6 = (f32[40,256]{1,0:T(8,128)S(1)}, f32[40,256]{1,0:T(8,128)}, u32[]{:S(2)}) copy-start(f32[40,256]{1,0:T(8,128)} %two_ref.1) | copy-start | bytes 122884
  39.1 32.0 %copy-start.7 = (f32[40,256]{1,0:T(8,128)S(1)}, f32[40,256]{1,0:T(8,128)}, u32[]{:S(2)}) copy-start(f32[40,256]{1,0:T(8,128)} %get-tuple-element.32.sum_ref) | copy-start | bytes 122884
  39.8 31.2 %copy-start.4 = (f32[40,256]{1,0:T(8,128)S(1)}, f32[40,256]{1,0:T(8,128)}, u32[]{:S(2)}) copy-start(f32[40,256]{1,0:T(8,128)} %master_ref.1) | copy-start | bytes 122884
  71.9 17.8 %copy-start.10 = (s32[4]{0:T(128)S(1)}, s32[4]{0:T(128)}, u32[]{:S(2)}) copy-start(s32[4]{0:T(128)} %len_ref) | copy-start | bytes 52
  71.9 31.2 %all-to-all-start.3 = ((bf16[8,40,256]{2,1,0:T(8,128)(2,1)}), bf16[8,40,256]{2,1,0:T(8,128)(2,1)S(1)}, u32[]{:S(2)}, u32[]{:S(2)}) async-start(bf16[8,40,256]{2,1,0:T(8,128)(2,1)} %get-tuple-element.35), calls=%async_computation.3 | async-start | bytes 327680 | tf_op jit(solution)/shard_map/all_to_all | solution.py:39
  89.8 3.6 %copy-start.11 = (f32[64]{0:T(128)S(1)}, f32[64]{0:T(128)}, u32[]{:S(2)}) copy-start(f32[64]{0:T(128)} %constant.2.clone) | copy-start | bytes 772
  89.8 13.2 %copy-start.9 = (bf16[256,320]{1,0:T(8,128)(2,1)S(1)}, bf16[256,320]{1,0:T(8,128)(2,1)}, u32[]{:S(2)}) copy-start(bf16[256,320]{1,0:T(8,128)(2,1)} %get-tuple-element.42) | copy-start | bytes 491524
  103.3 17.3 %copy-start.1 = (f32[96,128]{1,0:T(8,128)S(1)}, f32[96,128]{1,0:T(8,128)}, u32[]{:S(2)}) copy-start(f32[96,128]{1,0:T(8,128)} %get-tuple-element.47.acc_ref) | copy-start | bytes 147460
  103.3 17.3 %copy-start.2 = (f32[96,128]{1,0:T(8,128)S(1)}, f32[96,128]{1,0:T(8,128)}, u32[]{:S(2)}) copy-start(f32[96,128]{1,0:T(8,128)} %get-tuple-element.48.max_ref) | copy-start | bytes 147460
  103.3 17.3 %copy-start.3 = (f32[96,128]{1,0:T(8,128)S(1)}, f32[96,128]{1,0:T(8,128)}, u32[]{:S(2)}) copy-start(f32[96,128]{1,0:T(8,128)} %get-tuple-element.49.sum_ref) | copy-start | bytes 147460
  103.3 17.3 %copy-start.8 = (bf16[96,128]{1,0:T(8,128)(2,1)S(1)}, bf16[96,128]{1,0:T(8,128)(2,1)}, u32[]{:S(2)}) copy-start(bf16[96,128]{1,0:T(8,128)(2,1)} %get-tuple-element.46.q_ref) | copy-start | bytes 73732

commit v6 on v5

--- a/solution.py
+++ b/solution.py
@@ -21,8 +21,9 @@
 GRP_REP = ("g",) + REP
 SPLIT = ("zl", "g", "xl")
 ORDER = (5, 4, 0, 1, 2, 6, 7, 3)
-NORM_ORDER = tuple(zh * 8 + t for zh in ORDER for t in range(8))
 SPLIT_ORDER = tuple(range(15, -1, -1))
+SPLIT_CORE_ORDER = tuple(s * 2 + c for s in SPLIT_ORDER for c in range(2))
+NORM_ORDER = tuple(zh * 4 + y for zh in ORDER for y in range(4))
 QROWS = 24
 
 BETA_ONE = 0.9
@@ -53,30 +54,32 @@
     rest = squares - high
     middle = rest.astype(jnp.bfloat16).astype(jnp.float32)
     low = rest - middle
-    rows, steps, width = x_ref.shape
-    for r in range(rows):
-        flat_ref[pl.ds(r * steps, steps), :] = x_ref[r].astype(jnp.float32)
+    cores, width, steps = 2, x_ref.shape[2], x_ref.shape[1]
+    share = x_ref.shape[0] // cores
+    for r in range(share):
+        flat_ref[pl.ds(r * steps, steps), :] = x_ref[lax.axis_index("c") * share + r].astype(jnp.float32)
     step = width // (ZH * ZL * 4)
-    row = lax.broadcasted_iota(jnp.int32, (rows * steps, out_ref.shape[2] - ZH * step), 0)
-    terms = jnp.where(row == 0, high, jnp.where(row == 1, middle, jnp.where(row == 2, low, 0.0)))
+    room = (out_ref.shape[1], out_ref.shape[2] - ZH * step)
+    row, lane = lax.broadcasted_iota(jnp.int32, room, 0), lax.broadcasted_iota(jnp.int32, room, 1)
+    terms = jnp.where(lane == 0, high, jnp.where(lane == 1, middle, jnp.where(lane == 2, low, 0.0)))
+    terms = jnp.where(row == 0, terms, 0.0)
     for zl in range(ZL):
         for x in range(4):
             cols = []
             for zh in ORDER:
                 start = (((x // 2 * ZH + zh) * ZL + zl) * 2 + x % 2) * step
                 cols.append(flat_ref[:, start : start + step])
-            out_ref[SPLIT_ORDER.index(zl * 4 + x)] = jnp.concatenate(cols + [terms], axis=1).astype(jnp.bfloat16)
-
-
-def share_kernel(blocks_ref, squares_ref, inputs_ref):
-    n, tokens, _ = blocks_ref.shape
-    depth = inputs_ref.shape[1]
-    terms = blocks_ref[:, :, 256:384].astype(jnp.float32)
-    total = jnp.sum(jnp.sum(terms, axis=0), axis=0, keepdims=True)
-    total = jnp.broadcast_to(total[:, depth - 256 : depth - 255], (1, squares_ref.shape[2]))
+            block = jnp.concatenate(cols + [terms], axis=1).astype(jnp.bfloat16)
+            for c in range(cores):
+                out_ref[SPLIT_ORDER.index(zl * 4 + x) * cores + c] = block
+
+
+def share_kernel(blocks_ref, squares_ref, *, depth):
+    first = depth // HD * HD
+    terms = jnp.sum(blocks_ref[:, :, first : first + HD].astype(jnp.float32), axis=0)[:1, depth - first :]
+    total = terms[:, :1] + (terms[:, 1:2] + terms[:, 2:3])
     for i in range(squares_ref.shape[0]):
-        squares_ref[i] = total
-    inputs_ref[...] = blocks_ref[:, :, :depth].reshape(n * tokens, depth)
+        squares_ref[i] = jnp.broadcast_to(total, squares_ref.shape[1:])
 
 
 def update_kernel(squares_ref, sum_ref, master_ref, one_ref, two_ref, new_one_ref, new_two_ref, copies_ref):
@@ -171,23 +174,22 @@
         norm_kernel,
         out_shape=(
             jax.ShapeDtypeStruct((k_rows, col_width), jnp.float32),
-            jax.ShapeDtypeStruct((n_split, tokens, depth + 64), jnp.bfloat16),
+            jax.ShapeDtypeStruct((n_split * 2, tokens // 2, depth + 64), jnp.bfloat16),
         ),
         in_specs=[VMEM] * 2,
         out_specs=(VMEM,) * 2,
-        scratch_shapes=[pltpu.VMEM((tokens, model_width), jnp.float32)],
+        scratch_shapes=[pltpu.VMEM((tokens // 2, model_width), jnp.float32)],
     )(near(arrived), near(hidden_in))
-    squares, inputs = pl.pallas_call(
-        share_kernel,
-        out_shape=(
-            jax.ShapeDtypeStruct((ZH * n_tp, 1, HD), jnp.float32),
-            jax.ShapeDtypeStruct((n_split * tokens, depth), jnp.bfloat16),
-        ),
+    blocks = swapped(blocks, SPLIT + ("c",), [SPLIT_CORE_ORDER])
+    squares = pl.pallas_call(
+        functools.partial(share_kernel, depth=depth),
+        out_shape=jax.ShapeDtypeStruct((ZH * 4, 1, HD), jnp.float32),
         in_specs=[VMEM],
-        out_specs=(VMEM,) * 2,
-    )(near(swapped(blocks, SPLIT, [SPLIT_ORDER])))
-    inputs, squares, cache_lengths = lax.optimization_barrier((inputs, squares, cache_lengths))
-    squares = swapped(squares, ("zh",) + TP, [NORM_ORDER])
+        out_specs=VMEM,
+    )(near(blocks))
+    blocks, squares, cache_lengths = lax.optimization_barrier((blocks, squares, cache_lengths))
+    inputs = blocks[:, :, :depth].reshape(n_split * tokens, depth)
+    squares = swapped(squares, ("zh", "y"), [NORM_ORDER])
 
     q_rows, old_acc, old_max, old_sum = pl.pallas_call(
         cache_kernel,

time: 122 us -> 121 us (level)
  the two profiles are of different devices: /device:TPU:1 before, /device:TPU:2 now
where the time goes in v6:
time: 121 us
  blocking collectives  79.7 us (66%)
  starting transfers between devices  18.4 us (15%)
  waiting for transfers between devices  12.9 us (11%)
  Pallas kernels  7.32 us (6%)
  local copies, waits for them, and re-layouts  1.34 us (1%)
    all_to_all x4, blocking collectives, swapped(): lax.all_to_all(blocks, axes, split_axis=0, concat_axis=0, tiled=True, axi...  79.7 us
    all_to_all x1, starting transfers between devices, swapped(): lax.all_to_all(blocks, axes, split_axis=0, concat_axis=0, tiled=True, axi...  18.4 us
    all_to_all x1, waiting for transfers between devices, swapped(): lax.all_to_all(blocks, axes, split_axis=0, concat_axis=0, tiled=True, axi...  12.9 us
    pallas_call x1, Pallas kernels, body(): pl.pallas_call(cache_kernel, out_shape=(jax.ShapeDtypeStruct((all_q, HD),...  3.61 us
  transfers between devices with their start and end apart: 1, of which 1 were waited for; matrix products, arithmetic and copies ran while one was open for 0% of the time, Pallas kernels for 3%

profile of v6, /device:TPU:2, one launch (start us, length us, event | category | flops | bytes accessed | tf_op | source)
XLA Modules:
  0.0 120.8 jit_solution(16613572643842548161)
XLA Ops:
  0.6 1.1 copy.15
  1.7 0.1 copy.17
  1.8 0.0 copy-start
  1.8 12.6 %all_to_all.25.parts_ref = f32[8,40,256]{2,1,0:T(8,128)S(1)} all-to-all(f32[8,40,256]{2,1,0:T(8,128)S(1)} %bitcast.14), channel_id=1, replica_groups=mesh['g'=2,'zh'=8,'zl'=4,'xl'=2,'y'=4,'c'=2] {'y','c'}, dimensions={0} | all-to-all | bytes 655360 | tf_op jit(solution)/shard_map/all_to_all | solution.py:40
  14.5 0.0 copy-done
  14.5 0.9 shard_map.129
  15.4 23.4 %all_to_all.26.blocks_ref = bf16[32,8,384]{2,1,0:T(8,128)(2,1)S(1)} all-to-all(bf16[32,8,384]{2,1,0:T(8,128)(2,1)} %get-tuple-element.26), channel_id=1, replica_groups={{568,569,560,561,56,57,48,49,552,553,544,545,40,41,32,33,536,537,528,52..., dimensions={0} | all-to-all | bytes 393216 | tf_op jit(solution)/shard_map/all_to_all | solution.py:40
  38.8 0.0 copy-start.4
  38.8 0.0 copy-start.5
  38.8 0.0 copy-start.6
  38.8 0.0 copy-start.7
  38.8 0.9 shard_map.130
  39.7 30.0 %all_to_all.27.squares_ref = f32[32,1,128]{2,1,0:T(1,128)S(1)} all-to-all(f32[32,1,128]{2,1,0:T(1,128)} %shard_map.130), channel_id=1, replica_groups={{320,322,324,326,256,258,260,262,0,2,4,6,64,66,68,70,128,130,132,134,38..., dimensions={0} | all-to-all | bytes 32768 | tf_op jit(solution)/shard_map/all_to_all | solution.py:40
  69.7 0.0 copy-done.4
  69.7 0.0 copy-done.5
  69.7 0.0 copy-done.6
  69.7 0.0 copy-done.7
  69.7 0.8 shard_map.131
  70.5 0.0 copy-start.9
  70.5 18.4 %all-to-all-start.3 = ((bf16[8,40,256]{2,1,0:T(8,128)(2,1)}), bf16[8,40,256]{2,1,0:T(8,128)(2,1)S(1)}, u32[]{:S(2)}, u32[]{:S(2)}) async-start(bf16[8,40,256]{2,1,0:T(8,128)(2,1)} %get-tuple-element.31), calls=%async_computation.3 | async-start | bytes 327680 | tf_op jit(solution)/shard_map/all_to_all | solution.py:40
  88.9 0.0 copy-done.9
  88.9 0.1 add_convert_fusion
  89.0 0.1 convert_element_type.11
  89.0 0.0 copy-start.10
  89.0 3.6 %shard_map.132 = (bf16[96,128]{1,0:T(8,128)(2,1)}, f32[96,128]{1,0:T(8,128)}, f32[96,128]{1,0:T(8,128)}, f32[96,128]{1,0:T(8,128)}) custom-call(s32[4]{0:T(128)} %len_ref, bf16[4,4,640]{2,1,0:T(4,128)(2,1)} %q_ref.1, bf16[4,1024,128]{2,1,0:T(8,128)(2,1)} %k_ref.1, bf16[4,1024,128]{2,1,0:T(8,128)(2,1)} %v_ref.1), custom_call_target="tpu_custom_call" | custom-call | tf_op jit(solution)/shard_map/pallas_call | solution.py:194
  92.7 0.0 copy-done.10
  92.7 0.1 fusion
  92.8 0.1 pad_maximum_fusion
  92.9 12.9 %all-to-all-done.3 = bf16[8,40,256]{2,1,0:T(8,128)(2,1)S(1)} async-done(((bf16[8,40,256]{2,1,0:T(8,128)(2,1)}), bf16[8,40,256]{2,1,0:T(8,128)(2,1)S(1)}, u32[]{:S(2)}, u32[]{:S(2)}) %all-to-all-start.3) | async-done | bytes 163872 | tf_op jit(solution)/shard_map/all_to_all | solution.py:40
  105.8 0.2 fusion.1
  106.0 0.0 copy-start.1
  106.0 0.0 copy-start.2
  106.0 0.0 copy-start.3
  106.0 0.0 copy-start.8
  106.1 13.6 %all_to_all.28.part_ref = f32[16,16,256]{2,1,0:T(8,128)S(1)} all-to-all(f32[16,16,256]{2,1,0:T(8,128)S(1)} %fusion.1), channel_id=1, replica_groups={{568,560,56,48,552,544,40,32,536,528,24,16,520,512,8,0},{569,561,57,49,..., dimensions={0} | all-to-all | bytes 524288 | tf_op jit(solution)/shard_map/all_to_all | solution.py:40
  119.6 0.0 copy-done.1
  119.7 0.0 copy-done.2
  119.7 0.0 copy-done.3
  119.7 0.0 copy-done.8
  119.7 1.1 shard_map.133
  (1 shorter events, 0.0 us)
Async XLA Ops:
  1.8 12.7 %copy-start = (bf16[4,4,5120]{2,1,0:T(4,128)(2,1)S(1)}, bf16[4,4,5120]{2,1,0:T(4,128)(2,1)}, u32[]{:S(2)}) copy-start(bf16[4,4,5120]{2,1,0:T(4,128)(2,1)} %x_ref.1) | copy-start | bytes 491524
  38.8 30.9 %copy-start.4 = (f32[40,256]{1,0:T(8,128)S(1)}, f32[40,256]{1,0:T(8,128)}, u32[]{:S(2)}) copy-start(f32[40,256]{1,0:T(8,128)} %master_ref.1) | copy-start | bytes 122884
  38.8 30.9 %copy-start.5 = (f32[40,256]{1,0:T(8,128)S(1)}, f32[40,256]{1,0:T(8,128)}, u32[]{:S(2)}) copy-start(f32[40,256]{1,0:T(8,128)} %one_ref.1) | copy-start | bytes 122884
  38.8 30.9 %copy-start.6 = (f32[40,256]{1,0:T(8,128)S(1)}, f32[40,256]{1,0:T(8,128)}, u32[]{:S(2)}) copy-start(f32[40,256]{1,0:T(8,128)} %two_ref.1) | copy-start | bytes 122884
  38.8 30.9 %copy-start.7 = (f32[40,256]{1,0:T(8,128)S(1)}, f32[40,256]{1,0:T(8,128)}, u32[]{:S(2)}) copy-start(f32[40,256]{1,0:T(8,128)} %get-tuple-element.28.sum_ref) | copy-start | bytes 122884
  70.5 18.4 %copy-start.9 = (s32[4]{0:T(128)S(1)}, s32[4]{0:T(128)}, u32[]{:S(2)}) copy-start(s32[4]{0:T(128)} %len_ref) | copy-start | bytes 52
  70.5 35.3 %all-to-all-start.3 = ((bf16[8,40,256]{2,1,0:T(8,128)(2,1)}), bf16[8,40,256]{2,1,0:T(8,128)(2,1)S(1)}, u32[]{:S(2)}, u32[]{:S(2)}) async-start(bf16[8,40,256]{2,1,0:T(8,128)(2,1)} %get-tuple-element.31), calls=%async_computation.3 | async-start | bytes 327680 | tf_op jit(solution)/shard_map/all_to_all | solution.py:40
  89.0 3.6 %copy-start.10 = (f32[64]{0:T(128)S(1)}, f32[64]{0:T(128)}, u32[]{:S(2)}) copy-start(f32[64]{0:T(128)} %constant.2.clone) | copy-start | bytes 772
  106.0 13.6 %copy-start.1 = (f32[96,128]{1,0:T(8,128)S(1)}, f32[96,128]{1,0:T(8,128)}, u32[]{:S(2)}) copy-start(f32[96,128]{1,0:T(8,128)} %get-tuple-element.43.acc_ref) | copy-start | bytes 147460
  106.0 13.6 %copy-start.2 = (f32[96,128]{1,0:T(8,128)S(1)}, f32[96,128]{1,0:T(8,128)}, u32[]{:S(2)}) copy-start(f32[96,128]{1,0:T(8,128)} %get-tuple-element.44.max_ref) | copy-start | bytes 147460
  106.0 13.6 %copy-start.3 = (f32[96,128]{1,0:T(8,128)S(1)}, f32[96,128]{1,0:T(8,128)}, u32[]{:S(2)}) copy-start(f32[96,128]{1,0:T(8,128)} %get-tuple-element.45.sum_ref) | copy-start | bytes 147460
  106.0 13.6 %copy-start.8 = (bf16[96,128]{1,0:T(8,128)(2,1)S(1)}, bf16[96,128]{1,0:T(8,128)(2,1)}, u32[]{:S(2)}) copy-start(bf16[96,128]{1,0:T(8,128)(2,1)} %get-tuple-element.42.q_ref) | copy-start | bytes 73732

commit v7 on v6

--- a/solution.py
+++ b/solution.py
@@ -20,7 +20,7 @@
 REP = ("zh", "zl", "xl")
 GRP_REP = ("g",) + REP
 SPLIT = ("zl", "g", "xl")
-ORDER = (5, 4, 0, 1, 2, 6, 7, 3)
+ORDER = (5, 4, 0, 2, 1, 6, 7, 3)
 SPLIT_ORDER = tuple(range(15, -1, -1))
 SPLIT_CORE_ORDER = tuple(s * 2 + c for s in SPLIT_ORDER for c in range(2))
 NORM_ORDER = tuple(zh * 4 + y for zh in ORDER for y in range(4))

time: 121 us -> 121 us (level)
  the two profiles are of different devices: /device:TPU:2 before, /device:TPU:1 now
where the time goes in v7:
time: 121 us
  blocking collectives  83.9 us (69%)
  starting transfers between devices  18 us (15%)
  waiting for transfers between devices  9.14 us (8%)
  Pallas kernels  7.32 us (6%)
  local copies, waits for them, and re-layouts  1.34 us (1%)
    all_to_all x4, blocking collectives, swapped(): lax.all_to_all(blocks, axes, split_axis=0, concat_axis=0, tiled=True, axi...  83.9 us
    all_to_all x1, starting transfers between devices, swapped(): lax.all_to_all(blocks, axes, split_axis=0, concat_axis=0, tiled=True, axi...  18 us
    all_to_all x1, waiting for transfers between devices, swapped(): lax.all_to_all(blocks, axes, split_axis=0, concat_axis=0, tiled=True, axi...  9.14 us
    pallas_call x1, Pallas kernels, body(): pl.pallas_call(cache_kernel, out_shape=(jax.ShapeDtypeStruct((all_q, HD),...  3.61 us
  transfers between devices with their start and end apart: 1, of which 1 were waited for; matrix products, arithmetic and copies ran while one was open for 0% of the time, Pallas kernels for 3%

profile of v7, /device:TPU:1, one launch (start us, length us, event | category | flops | bytes accessed | tf_op | source)
XLA Modules:
  0.0 120.9 jit_solution(11289295458621885251)
XLA Ops:
  0.6 1.1 copy.15
  1.7 0.1 copy.17
  1.8 0.0 copy-start
  1.8 24.2 %all_to_all.25.parts_ref = f32[8,40,256]{2,1,0:T(8,128)S(1)} all-to-all(f32[8,40,256]{2,1,0:T(8,128)S(1)} %bitcast.14), channel_id=1, replica_groups=mesh['g'=2,'zh'=8,'zl'=4,'xl'=2,'y'=4,'c'=2] {'y','c'}, dimensions={0} | all-to-all | bytes 655360 | tf_op jit(solution)/shard_map/all_to_all | solution.py:40
  26.0 0.0 copy-done
  26.0 0.9 shard_map.129
  26.9 14.1 %all_to_all.26.blocks_ref = bf16[32,8,384]{2,1,0:T(8,128)(2,1)S(1)} all-to-all(bf16[32,8,384]{2,1,0:T(8,128)(2,1)} %get-tuple-element.26), channel_id=1, replica_groups={{568,569,560,561,56,57,48,49,552,553,544,545,40,41,32,33,536,537,528,52..., dimensions={0} | all-to-all | bytes 393216 | tf_op jit(solution)/shard_map/all_to_all | solution.py:40
  41.0 0.0 copy-start.4
  41.0 0.0 copy-start.5
  41.0 0.0 copy-start.6
  41.1 0.0 copy-start.7
  41.1 0.9 shard_map.130
  41.9 28.6 %all_to_all.27.squares_ref = f32[32,1,128]{2,1,0:T(1,128)S(1)} all-to-all(f32[32,1,128]{2,1,0:T(1,128)} %shard_map.130), channel_id=1, replica_groups={{320,322,324,326,256,258,260,262,0,2,4,6,128,130,132,134,64,66,68,70,38..., dimensions={0} | all-to-all | bytes 32768 | tf_op jit(solution)/shard_map/all_to_all | solution.py:40
  70.5 0.0 copy-done.4
  70.5 0.0 copy-done.5
  70.5 0.0 copy-done.6
  70.5 0.0 copy-done.7
  70.5 0.8 shard_map.131
  71.3 0.0 copy-start.9
  71.3 18.0 %all-to-all-start.3 = ((bf16[8,40,256]{2,1,0:T(8,128)(2,1)}), bf16[8,40,256]{2,1,0:T(8,128)(2,1)S(1)}, u32[]{:S(2)}, u32[]{:S(2)}) async-start(bf16[8,40,256]{2,1,0:T(8,128)(2,1)} %get-tuple-element.31), calls=%async_computation.3 | async-start | bytes 327680 | tf_op jit(solution)/shard_map/all_to_all | solution.py:40
  89.3 0.0 copy-done.9
  89.3 0.1 add_convert_fusion
  89.4 0.1 convert_element_type.11
  89.5 0.0 copy-start.10
  89.5 3.6 %shard_map.132 = (bf16[96,128]{1,0:T(8,128)(2,1)}, f32[96,128]{1,0:T(8,128)}, f32[96,128]{1,0:T(8,128)}, f32[96,128]{1,0:T(8,128)}) custom-call(s32[4]{0:T(128)} %len_ref, bf16[4,4,640]{2,1,0:T(4,128)(2,1)} %q_ref.1, bf16[4,1024,128]{2,1,0:T(8,128)(2,1)} %k_ref.1, bf16[4,1024,128]{2,1,0:T(8,128)(2,1)} %v_ref.1), custom_call_target="tpu_custom_call" | custom-call | tf_op jit(solution)/shard_map/pallas_call | solution.py:194
  93.1 0.0 copy-done.10
  93.1 0.1 fusion
  93.2 0.1 pad_maximum_fusion
  93.3 9.1 %all-to-all-done.3 = bf16[8,40,256]{2,1,0:T(8,128)(2,1)S(1)} async-done(((bf16[8,40,256]{2,1,0:T(8,128)(2,1)}), bf16[8,40,256]{2,1,0:T(8,128)(2,1)S(1)}, u32[]{:S(2)}, u32[]{:S(2)}) %all-to-all-start.3) | async-done | bytes 163872 | tf_op jit(solution)/shard_map/all_to_all | solution.py:40
  102.5 0.2 fusion.1
  102.7 0.0 copy-start.1
  102.7 0.0 copy-start.2
  102.7 0.0 copy-start.3
  102.7 0.0 copy-start.8
  102.7 17.0 %all_to_all.28.part_ref = f32[16,16,256]{2,1,0:T(8,128)S(1)} all-to-all(f32[16,16,256]{2,1,0:T(8,128)S(1)} %fusion.1), channel_id=1, replica_groups={{568,560,56,48,552,544,40,32,536,528,24,16,520,512,8,0},{569,561,57,49,..., dimensions={0} | all-to-all | bytes 524288 | tf_op jit(solution)/shard_map/all_to_all | solution.py:40
  119.7 0.0 copy-done.1
  119.7 0.0 copy-done.2
  119.7 0.0 copy-done.3
  119.8 0.0 copy-done.8
  119.8 1.1 shard_map.133
  (1 shorter events, 0.0 us)
Async XLA Ops:
  1.8 24.2 %copy-start = (bf16[4,4,5120]{2,1,0:T(4,128)(2,1)S(1)}, bf16[4,4,5120]{2,1,0:T(4,128)(2,1)}, u32[]{:S(2)}) copy-start(bf16[4,4,5120]{2,1,0:T(4,128)(2,1)} %x_ref.1) | copy-start | bytes 491524
  41.0 29.4 %copy-start.4 = (f32[40,256]{1,0:T(8,128)S(1)}, f32[40,256]{1,0:T(8,128)}, u32[]{:S(2)}) copy-start(f32[40,256]{1,0:T(8,128)} %master_ref.1) | copy-start | bytes 122884
  41.0 29.4 %copy-start.5 = (f32[40,256]{1,0:T(8,128)S(1)}, f32[40,256]{1,0:T(8,128)}, u32[]{:S(2)}) copy-start(f32[40,256]{1,0:T(8,128)} %one_ref.1) | copy-start | bytes 122884
  41.0 29.4 %copy-start.6 = (f32[40,256]{1,0:T(8,128)S(1)}, f32[40,256]{1,0:T(8,128)}, u32[]{:S(2)}) copy-start(f32[40,256]{1,0:T(8,128)} %two_ref.1) | copy-start | bytes 122884
  41.1 29.4 %copy-start.7 = (f32[40,256]{1,0:T(8,128)S(1)}, f32[40,256]{1,0:T(8,128)}, u32[]{:S(2)}) copy-start(f32[40,256]{1,0:T(8,128)} %get-tuple-element.28.sum_ref) | copy-start | bytes 122884
  71.3 18.0 %copy-start.9 = (s32[4]{0:T(128)S(1)}, s32[4]{0:T(128)}, u32[]{:S(2)}) copy-start(s32[4]{0:T(128)} %len_ref) | copy-start | bytes 52
  71.3 31.2 %all-to-all-start.3 = ((bf16[8,40,256]{2,1,0:T(8,128)(2,1)}), bf16[8,40,256]{2,1,0:T(8,128)(2,1)S(1)}, u32[]{:S(2)}, u32[]{:S(2)}) async-start(bf16[8,40,256]{2,1,0:T(8,128)(2,1)} %get-tuple-element.31), calls=%async_computation.3 | async-start | bytes 327680 | tf_op jit(solution)/shard_map/all_to_all | solution.py:40
  89.5 3.6 %copy-start.10 = (f32[64]{0:T(128)S(1)}, f32[64]{0:T(128)}, u32[]{:S(2)}) copy-start(f32[64]{0:T(128)} %constant.2.clone) | copy-start | bytes 772
  102.7 17.1 %copy-start.1 = (f32[96,128]{1,0:T(8,128)S(1)}, f32[96,128]{1,0:T(8,128)}, u32[]{:S(2)}) copy-start(f32[96,128]{1,0:T(8,128)} %get-tuple-element.43.acc_ref) | copy-start | bytes 147460
  102.7 17.1 %copy-start.2 = (f32[96,128]{1,0:T(8,128)S(1)}, f32[96,128]{1,0:T(8,128)}, u32[]{:S(2)}) copy-start(f32[96,128]{1,0:T(8,128)} %get-tuple-element.44.max_ref) | copy-start | bytes 147460
  102.7 17.0 %copy-start.3 = (f32[96,128]{1,0:T(8,128)S(1)}, f32[96,128]{1,0:T(8,128)}, u32[]{:S(2)}) copy-start(f32[96,128]{1,0:T(8,128)} %get-tuple-element.45.sum_ref) | copy-start | bytes 147460
  102.7 17.0 %copy-start.8 = (bf16[96,128]{1,0:T(8,128)(2,1)S(1)}, bf16[96,128]{1,0:T(8,128)(2,1)}, u32[]{:S(2)}) copy-start(bf16[96,128]{1,0:T(8,128)(2,1)} %get-tuple-element.42.q_ref) | copy-start | bytes 73732
